TPU v7x, 128 devices: a whole 4x4x4 slice. The times are simulated.
128 devices in a mesh: ta: 16 (over y, x_lo, core), sa: 8 (over x_hi, z).
Axes of the slice: x: 4 (x_hi: 2, x_lo: 2; x = x_hi * 2 + x_lo), y: 4, z: 4, core: 2. Of those that a mesh axis runs over, the one named last changes fastest.
Arguments:
- propagators: bfloat16 [16, 288, 131072], P('ta', None, 'sa'), may hold values from -6 to 6
- z_sites: int32 [65536], P(('ta', 'sa')), may hold values from 0 to 1023
- z_class: int32 [65536], P(('ta', 'sa')), may hold values from 0 to 31
- kernel_table: float32 [4, 32], replicated, may hold values from -0.00030517578 to 0.00030517578
- pair_combo: int32 [65536, 1], P(('ta', 'sa')), may hold values from 0 to 1023; in each aligned block of 512 rows (0 to 511, 512 to 1023, ...) at most 2 rows name the same one
- pair_site: int32 [65536], P(('ta', 'sa')), may hold values from 0 to 1023
Outputs:
- amplitudes: float32 [2, 65536], P(None, ('ta', 'sa'))
Inputs may be any that keep to these rules, and one draw needn't show every extreme that they name: `pair_combo`: in each block of 512 pairs (the pairs of one slab block) no combination is named by more than 2 pairs, a bound that some block reaches.
All inputs are finite; a program needn't handle non-finite values.
Results may differ from a plain program's by a relative error of at most 0.0012.
Values may be sent and summed in bfloat16 or wider, within the bound.
No kernel may reach another device: no remote copies, remote signals or barrier semaphores. Data moves between devices by JAX's collectives and lax.ppermute only.
A program may use at most 192 MiB of HBM per device.

v0:
```python
import jax
import jax.numpy as jnp
from jax import lax
from jax.sharding import PartitionSpec as P

NCOMB = 1024
CAP = 2


def trace_pair(combo_mat, prop_mat):
    combo_four = combo_mat.reshape(-1, 2, 12, 12)
    prop_four = jnp.swapaxes(prop_mat.astype(jnp.float32).reshape(-1, 2, 12, 12), 2, 3)
    real_part = jnp.sum(
        combo_four[:, 0] * prop_four[:, 0] - combo_four[:, 1] * prop_four[:, 1], axis=(1, 2)
    )
    imag_part = jnp.sum(
        combo_four[:, 0] * prop_four[:, 1] + combo_four[:, 1] * prop_four[:, 0], axis=(1, 2)
    )
    return jnp.stack([real_part, imag_part])


def site_sums(z_rows, weights, class_count, source_count, z_count):
    shaped = z_rows.reshape(source_count, 2, 12, 12, z_count)
    left_rows = jnp.transpose(shaped, (0, 3, 1, 2, 4))
    weighted = (weights[:, None, None, None, None, :] * left_rows[None].astype(jnp.float32)).astype(
        jnp.bfloat16
    )
    weighted = weighted.reshape(class_count * source_count * 12, 24 * z_count)
    right_rows = jnp.transpose(shaped, (1, 2, 4, 0, 3))
    swapped = jnp.stack([right_rows[1], -right_rows[0]], axis=0)
    extended = jnp.stack([right_rows, swapped], axis=4).reshape(24 * z_count, source_count * 24)
    product = jnp.dot(weighted, extended, preferred_element_type=jnp.float32)
    product = product.reshape(class_count, source_count, 12, source_count, 2, 12)
    return jnp.transpose(product, (0, 3, 1, 4, 2, 5)).reshape(-1, 288)


def local(propagators, z_sites, z_class, kernel_table, pair_combo, pair_site):
    slab_count = lax.axis_size("ta")
    device_count = slab_count * lax.axis_size("sa")
    source_count = propagators.shape[0] * slab_count
    z_count = z_sites.shape[0]
    pair_count = pair_site.shape[0]
    slab_rows = lax.all_to_all(propagators, "ta", split_axis=2, concat_axis=0, tiled=True)
    z_rows = jnp.take(slab_rows, z_sites, axis=2)
    partner_rows = jnp.take(slab_rows, pair_site, axis=2)
    class_count = kernel_table.shape[0]
    one_hot = (
        z_class[None, :] == jnp.arange(kernel_table.shape[1], dtype=jnp.int32)[:, None]
    ).astype(jnp.float32)
    weights = jnp.dot(kernel_table, one_hot, precision=lax.Precision.HIGHEST)
    partial_sums = site_sums(z_rows, weights, class_count, source_count, z_count)
    combo_ids = pair_combo[:, 0]
    source_ids = combo_ids // source_count % source_count
    counter = jnp.arange(pair_count, dtype=jnp.int32)
    partner_mats = partner_rows[source_ids, :, counter]
    owned_sums = lax.psum_scatter(partial_sums, ("ta", "sa"), scatter_dimension=0, tiled=True)
    earlier = (combo_ids[:, None] == combo_ids[None, :]) & (counter[None, :] < counter[:, None])
    ranking = jnp.sum(earlier.astype(jnp.int32), axis=1)
    slot_ids = combo_ids * CAP + ranking
    outgoing = jnp.zeros((NCOMB * CAP, 288), jnp.bfloat16).at[slot_ids].set(partner_mats)
    received = lax.all_to_all(
        outgoing.reshape(device_count, -1, 288),
        ("ta", "sa"),
        split_axis=0,
        concat_axis=0,
        tiled=True,
    )
    repeated = jnp.repeat(owned_sums, CAP, axis=0)
    broadcast_sums = jnp.broadcast_to(repeated[None], received.shape).reshape(-1, 288)
    results = trace_pair(broadcast_sums, received.reshape(-1, 288)).reshape(2, device_count, -1)
    returned = lax.all_to_all(results, ("ta", "sa"), split_axis=1, concat_axis=1, tiled=True)
    return returned.reshape(2, -1)[:, slot_ids]


def solution(mesh):
    placed = (
        P("ta", None, "sa"),
        P(("ta", "sa")),
        P(("ta", "sa")),
        P(),
        P(("ta", "sa"), None),
        P(("ta", "sa")),
    )
    return jax.shard_map(
        local, mesh=mesh, in_specs=placed, out_specs=P(None, ("ta", "sa")), check_vma=False
    )
```

profile of v0, /device:TPU:1, one launch (start us, length us, event | category | flops | bytes accessed | tf_op | source)
XLA Modules:
  0.0 1007.1 jit_solution(6629894194401765139)
XLA Ops:
  6.5 50.5 %copy.82 = bf16[1,288,16384]{1,0,2:T(2,128)(2,1)} copy(bf16[1,288,16384]{2,1,0:T(8,128)(2,1)} %param.8) | data formatting | bytes 18874368 | tf_op args[0]
  57.0 0.5 broadcast.99
  57.5 268.2 %reduce.2 = bf16[16384,288]{1,0:T(8,128)(2,1)} reduce(bf16[16384,1,288]{2,1,0:T(2,128)(2,1)} %bitcast.65, bf16[]{:T(256)} %broadcast.99), dimensions={1}, to_apply=%bitcast.54.reduce_sub_computation | reduce | bytes 18874370
  325.7 21.8 %reshape.119 = bf16[16,2,147456]{2,1,0:T(2,128)(2,1)} reshape(bf16[16384,288]{1,0:T(8,128)(2,1)} %reduce.2) | data formatting | bytes 18874368
  347.5 7.4 all-to-all-start
  354.9 0.1 convolution_bitcast_fusion
  355.1 0.1 mul.49
  355.3 0.3 convert_reduce_fusion
  355.6 105.0 %all-to-all-done = bf16[16,2,147456]{2,1,0:T(2,128)(2,1)} async-done(((bf16[16,2,147456]{2,1,0:T(2,128)(2,1)}), bf16[16,2,147456]{2,1,0:T(2,128)(2,1)}, u32[]{:S(2)}, u32[]{:S(2)}) %all-to-all-start) | async-done | bytes 9437216 | tf_op jit(solution)/shard_map/all_to_all | solution.py:43
  460.6 24.9 %reshape.120 = bf16[16384,1,288]{2,1,0:T(2,128)(2,1)} reshape(bf16[16,2,147456]{2,1,0:T(2,128)(2,1)} %all-to-all-done) | data formatting | bytes 18874368
  485.5 11.5 %copy.107 = bf16[1,288,16384]{1,2,0:T(8,128)(2,1)S(1)} copy(bf16[1,288,16384]{1,0,2:T(2,128)(2,1)} %bitcast.66) | data formatting | bytes 18874368
  497.1 36.9 %copy.115 = bf16[1,288,16,1024]{1,2,3,0:T(8,128)(2,1)} copy(bf16[1,288,16,1024]{1,3,2,0:T(8,128)(2,1)S(1)} %bitcast.70) | data formatting | bytes 18874368 | tf_op jit(solution)/shard_map/all_to_all | solution.py:43
  534.0 8.8 gather_fusion.2
  542.8 8.8 gather_fusion.1
  551.5 7.6 select_bitcast_fusion.1
  559.2 9.4 copy.85
  568.5 4.4 select_bitcast_fusion
  573.0 4.1 copy.92
  577.1 7.5 scatter_custom_fusion
  584.5 9.3 all-to-all-start.1
  593.9 2.7 fusion.20
  596.6 2.5 maximum_bitcast_fusion
  599.1 8.2 pad_maximum_fusion
  607.3 13.0 %copy.87 = bf16[2,12,512,16,2,12]{2,1,0,5,4,3:T(8,128)(2,1)} copy(bf16[2,12,512,16,2,12]{2,3,5,1,0,4:T(8,128)(2,1)} %pad_maximum_fusion) | data formatting | bytes 18874368 | tf_op jit(solution)/shard_map/stack | solution.py:31
  620.2 15.7 %reshape.58 = bf16[12288,384]{0,1:T(8,128)(2,1)} reshape(bf16[2,12,512,16,2,12]{2,1,0,5,4,3:T(8,128)(2,1)} %copy.87) | data formatting | bytes 18874368 | tf_op jit(solution)/shard_map/reshape | solution.py:31
  636.0 13.7 %dot_general.15 = bf16[16,2,12,12288]{3,2,1,0:T(8,128)(2,1)} reshape(bf16[384,12288]{1,0:T(8,128)(2,1)} %bitcast.73) | data formatting | bytes 18874368 | tf_op jit(solution)/shard_map/dot_general | solution.py:32
  649.6 3.7 convert_bitcast_fusion
  653.3 11.2 %copy.86 = f32[16,12,2,12,512]{4,3,2,0,1:T(8,128)} copy(f32[16,12,2,12,512]{4,0,1,3,2:T(8,128)S(1)} %convert_bitcast_fusion) | data formatting | bytes 18874368 | tf_op jit(solution)/shard_map/mul | solution.py:25
  664.5 11.1 %reshape.62 = f32[16,12,12288]{2,0,1:T(8,128)} reshape(f32[16,12,2,12,512]{4,3,2,0,1:T(8,128)} %copy.86) | data formatting | bytes 18874368 | tf_op jit(solution)/shard_map/mul | solution.py:25
  675.6 12.4 %fusion.25 = bf16[4,16,12,12288,1,1]{3,1,5,4,2,0:T(8,128)(2,1)} fusion(f32[16,12,12288]{2,0,1:T(8,128)} %reshape.62, f32[4,12288]{1,0:T(4,128)S(1)} %mul.49), kind=kLoop, calls=%fused_computation.6.clone.clone.clone.clone.1 | loop fusion | flops 18874368 | bytes 28508160 | tf_op jit(solution)/shard_map/dot_general | solution.py:32
  688.0 66.4 %fusion.6 = f32[4,16,16,2,12,12]{1,2,5,3,4,0:T(8,128)} fusion(bf16[16,2,12,12288,1,1]{3,2,1,0,5,4:T(8,128)(2,1)} %bitcast.75, bf16[4,16,12,12288,1,1]{3,1,5,4,2,0:T(8,128)(2,1)} %fusion.25), kind=kOutput, calls=%fused_computation.17 | convolution fusion | flops 7247757312 | bytes 29491200 | tf_op jit(solution)/shard_map/dot_general | solution.py:32
  754.4 9.7 copy.89
  764.1 9.3 reshape.59
  773.4 149.3 %all-reduce.3.cloned.1.call-done = f32[1024,288]{0,1:T(8,128)} async-done(((f32[1024,288]{0,1:T(8,128)}), f32[1024,288]{0,1:T(8,128)}) %all-reduce.3.cloned.1.call-update) | async-done | bytes 1179664
  922.7 1.0 constant_dynamic-slice_fusion
  923.9 7.7 broadcast_in_dim.19
  931.6 14.9 %reshape_reshape.3 = f32[2048,2,12,12]{0,3,2,1:T(8,128)S(1)} reshape(f32[128,16,288]{1,0,2:T(8,128)} %broadcast_in_dim.19) | data formatting | bytes 4718592 | tf_op jit(solution)/shard_map/reshape;reshape | solution.py:11
  946.5 2.7 copy.93
  949.2 10.4 %copy.94 = f32[128,16,288]{1,0,2:T(8,128)} copy(bf16[128,16,288]{0,2,1:T(8,128)(2,1)} %copy.93) | data formatting | bytes 3538944 | tf_op jit(solution)/shard_map/transpose | solution.py:12
  959.6 16.2 %reshape.63 = f32[2048,2,12,12]{0,3,2,1:T(8,128)} reshape(f32[128,16,288]{1,0,2:T(8,128)} %copy.94) | data formatting | bytes 4718592 | tf_op jit(solution)/shard_map/transpose | solution.py:12
  975.8 3.3 copy.116
  979.1 0.8 subtract_reduce_fusion
  980.0 0.7 copy.96
  980.8 6.5 all-to-all-start.2
  987.3 9.9 all-to-all-done.2
  997.2 0.8 copy.97
  998.0 1.0 gather_fusion
  999.1 0.7 copy.98
  (35 shorter events, 0.6 us)
Async XLA Ops:
  6.5 348.4 %copy-start = (f32[4,32]{1,0:T(4,128)S(1)}, f32[4,32]{1,0:T(4,128)}, u32[]{:S(2)}) copy-start(f32[4,32]{1,0:T(4,128)} %param.11) | copy-start | bytes 1540
  347.5 7.4 copy-start.7
  347.5 7.8 copy-start.3
  347.5 7.8 copy-start.4
  347.5 7.8 copy-start.2
  347.5 113.1 %all-to-all-start = ((bf16[16,2,147456]{2,1,0:T(2,128)(2,1)}), bf16[16,2,147456]{2,1,0:T(2,128)(2,1)}, u32[]{:S(2)}, u32[]{:S(2)}) async-start(bf16[16,2,147456]{2,1,0:T(2,128)(2,1)} %reshape.119), calls=%async_computation | async-start | bytes 18874368 | tf_op jit(solution)/shard_map/all_to_all | solution.py:43
  355.6 221.4 %copy-start.5 = (s32[512,1]{0,1:T(1,128)}, s32[512,1]{0,1:T(1,128)S(1)}, u32[]{:S(2)}) copy-start(s32[512,1]{0,1:T(1,128)S(1)} %get-tuple-element.11) | copy-start | bytes 6148
  584.5 362.0 %all-to-all-start.1 = ((bf16[128,16,288]{2,1,0:T(8,128)(2,1)}), bf16[128,16,288]{2,1,0:T(8,128)(2,1)}, u32[]{:S(2)}, u32[]{:S(2)}) async-start(bf16[128,16,288]{2,1,0:T(8,128)(2,1)} %bitcast.21), calls=%async_computation.1 | async-start | bytes 3145728 | tf_op jit(solution)/shard_map/all_to_all | solution.py:61
  593.8 328.8 %all-reduce.3.cloned.1.call-start = ((), (), s32[]{:S(2)}) async-start(), calls=%async_computation.3 | async-start | bytes 2359296
  959.6 40.2 %copy-start.1 = (f32[4,32]{1,0:T(4,128)S(1)}, f32[4,32]{1,0:T(4,128)}, u32[]{:S(2)}) copy-start(f32[4,32]{1,0:T(4,128)} %param.11) | copy-start | bytes 1540
  975.8 11.5 %copy-start.6 = (s32[512,1]{0,1:T(1,128)S(1)}, s32[512,1]{0,1:T(1,128)}, u32[]{:S(2)}) copy-start(s32[512,1]{0,1:T(1,128)} %copy-done.5) | copy-start | bytes 6148
  980.8 16.4 %all-to-all-start.2 = ((f32[2,128,16]{2,0,1:T(2,128)}), f32[2,128,16]{2,0,1:T(2,128)S(1)}, u32[]{:S(2)}, u32[]{:S(2)}) async-start(f32[2,128,16]{2,0,1:T(2,128)} %copy.96), calls=%async_computation.2 | async-start | bytes 262144 | tf_op jit(solution)/shard_map/all_to_all | solution.py:71
Sparse Core Ops, SparseCore 0:
  773.5 149.1 all-reduce.2
where the time goes:
time: 1020 us; the launch traced here: 1010 us
  local copies, waits for them, and re-layouts  328 us (32%)
  other arithmetic  311 us (30%)
  waiting for transfers between devices  264 us (26%)
  matrix products  66.6 us (7%)
  starting transfers between devices  23.2 us (2%)
  between operations  14.1 us (1%)
    unnamed x1, other arithmetic  268 us
    unnamed x2, waiting for transfers between devices  149 us
    unnamed x22, local copies, waits for them, and re-layouts  110 us
    all_to_all x1, waiting for transfers between devices, local(): lax.all_to_all(propagators, 'ta', split_axis=2, concat_axis=0, tiled=True)  105 us
    dot_general x1, matrix products, site_sums(): product = jnp.dot(weighted, extended, preferred_element_type=jnp.float32)  66.4 us
    all_to_all x1, local copies, waits for them, and re-layouts, local(): lax.all_to_all(propagators, 'ta', split_axis=2, concat_axis=0, tiled=True)  36.9 us
    transpose x3, local copies, waits for them, and re-layouts, trace_pair(): jnp.swapaxes(prop_mat.astype(jnp.float32).reshape(-1, 2, 12, 12), 2, 3)  29.8 us
    mul x4, local copies, waits for them, and re-layouts, site_sums(): weights[:, None, None, None, None, :] * left_rows[None].astype(jnp.float32)  22.5 us
  transfers between devices with their start and end apart: 4, of which 3 were waited for; matrix products, arithmetic and copies ran while one was open for 20% of the time, Pallas kernels for 0%

commit v1 on v0

v1 whole, which is shorter than its diff:
```python
import jax
import jax.numpy as jnp
import numpy as np
from jax import lax
from jax.experimental import pallas as pl
from jax.experimental.pallas import tpu as pltpu
from jax.sharding import PartitionSpec as P

NSC = 12
VMEM = 56 * 1024 * 1024


def one_hot_columns(idx_row, count):
    rows = lax.broadcasted_iota(jnp.int32, (count, idx_row.shape[1]), 0)
    return jnp.where(rows == idx_row, 1.0, 0.0).astype(jnp.bfloat16)


def pick_sites(props, idx, first_row):
    hot = jnp.concatenate(
        [one_hot_columns(idx[r : r + 1, :], props.shape[1]) for r in range(first_row, first_row + 4)],
        axis=1,
    )
    return jnp.dot(props, hot, preferred_element_type=jnp.float32)


def z_gather_kernel(idx_ref, props_ref, out_ref):
    picked = pick_sites(props_ref[0], idx_ref[0], 0)
    count = picked.shape[1]
    half = NSC * NSC
    for l in range(NSC):
        re, im = l * NSC, half + l * NSC
        out_ref[0, :, l * count : (l + 1) * count] = jnp.concatenate(
            [picked[re : re + 8], picked[im : im + 8], picked[re + 8 : re + 12], picked[im + 8 : im + 12]],
            axis=0,
        ).astype(jnp.bfloat16)


def pair_gather_kernel(idx_ref, props_ref, out_ref):
    out_ref[...] = pick_sites(props_ref[0], idx_ref[0], 4).astype(jnp.bfloat16)


def combo_kernel(x_ref, w_ref, out_ref, acc_ref):
    step = pl.program_id(0)
    sources, _, depth = x_ref.shape
    wide = x_ref[...].astype(jnp.float32)
    rows = jnp.concatenate(
        [wide[:, 8 * t : 8 * t + 8, :].reshape(sources * 8, depth) for t in range(3)], axis=0
    )
    right = rows.astype(jnp.bfloat16)
    classes = w_ref.shape[0]
    for c in range(classes):
        left = (rows * w_ref[c : c + 1, :]).astype(jnp.bfloat16)
        part = lax.dot_general(
            right, left, (((1,), (1,)), ((), ())), preferred_element_type=jnp.float32
        )

        @pl.when(step == 0)
        def _():
            acc_ref[c] = part

        @pl.when(step > 0)
        def _():
            acc_ref[c] += part

    @pl.when(step == pl.num_programs(0) - 1)
    def _():
        n = sources * 8
        low_row = lax.broadcasted_iota(jnp.int32, (n, n), 0) % 8 < 4
        low_lane = lax.broadcasted_iota(jnp.int32, (n, n), 1) % 8 < 4

        def swap_rows(m):
            return pltpu.roll(m.reshape(sources, 8, n), 4, 1).reshape(n, n)

        for c in range(classes):
            def blk(i, j):
                return acc_ref[c, n * i : n * i + n, n * j : n * j + n]

            re = blk(0, 0) + blk(1, 1)
            im = blk(1, 0) - blk(0, 1)
            a, b = blk(0, 2), blk(1, 2)
            wide_col = jnp.where(low_lane, a + pltpu.roll(b, n - 4, 1), pltpu.roll(b, 4, 1) - a)
            a, b = blk(2, 0), swap_rows(blk(2, 1))
            tall_row = jnp.where(low_row, a + b, a - b)
            a = blk(2, 2)
            b = swap_rows(pltpu.roll(a, n - 4, 1))
            corner = jnp.where(low_lane, jnp.where(low_row, a + b, a - b), 0.0)
            for k, m in enumerate((re, im, wide_col, tall_row, corner)):
                at = (c * 5 + k) * 8
                out_ref[:, at : at + 8, :] = m.reshape(sources, 8, n)


def spread_matrix():
    out = np.zeros((5, 8, 8, 768), np.float32)

    def put(k, r, q, j, i, imag):
        at = j * NSC + i
        half = NSC * NSC
        if imag:
            out[k, r, q, half + at] = -1.0
            out[k, r, q, 384 + at] = 1.0
        else:
            out[k, r, q, at] = 1.0
            out[k, r, q, 384 + half + at] = 1.0

    for r in range(8):
        for q in range(8):
            put(0, r, q, r, q, False)
            put(1, r, q, r, q, True)
            put(2, r, q, r, 8 + q % 4, q >= 4)
            put(3, r, q, 8 + r % 4, q, r >= 4)
            if q < 4:
                put(4, r, q, 8 + r % 4, 8 + q, r >= 4)
    return out.reshape(320, 768)


def fold_matrix():
    r = np.arange(1024)[:, None] // 128
    q = np.arange(1024)[:, None] % 8
    return (np.arange(64)[None, :] == r * 8 + q).astype(np.float32)


def amplitude_kernel(sums_ref, fold_ref, spread_ref, key_ref, partner_ref, out_ref, q_ref):
    classes, sources = 4, 16

    @pl.when(pl.program_id(0) == 0)
    def _():
        sums = jnp.sum(sums_ref[...], axis=0)
        own = (
            lax.broadcasted_iota(jnp.int32, (sources, 128), 1) // 8
            == lax.broadcasted_iota(jnp.int32, (sources, 128), 0)
        )
        total = jnp.zeros((2 * classes * sources, 768), jnp.float32)
        for k in range(5):
            tall = []
            for c in range(classes):
                at = (c * 5 + k) * 8
                tall.append(
                    jnp.concatenate(
                        [
                            jnp.where(own, jnp.broadcast_to(sums[at + r : at + r + 1, :], (sources, 128)), 0.0)
                            for r in range(8)
                        ],
                        axis=1,
                    )
                )
            tall = jnp.concatenate(tall, axis=0)
            high = tall.astype(jnp.bfloat16)
            low = (tall - high.astype(jnp.float32)).astype(jnp.bfloat16)
            both = jnp.concatenate([high, low], axis=0)
            folded = jnp.dot(both, fold_ref[...], preferred_element_type=jnp.float32)
            total += jnp.dot(
                folded.astype(jnp.bfloat16),
                spread_ref[64 * k : 64 * k + 64, :],
                preferred_element_type=jnp.float32,
            )
        q_ref[0:128, :] = total[:, 0:288].astype(jnp.bfloat16)
        q_ref[128:256, :] = total[:, 384:672].astype(jnp.bfloat16)

    traces = jnp.dot(q_ref[...], partner_ref[...], preferred_element_type=jnp.float32)
    combos = classes * sources
    here = lax.broadcasted_iota(jnp.int32, (combos, 128), 0)
    blocks, _, count = key_ref.shape
    for u in range(blocks):
        for g in range(count // 128):
            lanes = slice(u * count + g * 128, u * count + g * 128 + 128)
            mask = here == key_ref[u, :, g * 128 : g * 128 + 128]
            for part in range(2):
                at = part * 2 * combos
                value = traces[at : at + combos, lanes] + traces[at + combos : at + 2 * combos, lanes]
                out_ref[u, part : part + 1, g * 128 : g * 128 + 128] = jnp.sum(
                    jnp.where(mask, value, 0.0), axis=0, keepdims=True
                )


def params():
    return pltpu.CompilerParams(vmem_limit_bytes=VMEM)


def local(propagators, z_sites, z_class, kernel_table, pair_combo, pair_site):
    slabs = lax.axis_size("ta")
    blocks = lax.axis_size("sa")
    me = lax.axis_index("ta")
    rows = propagators.shape[1]
    site_count = propagators.shape[2] // slabs
    z_count = z_sites.shape[0]
    pair_count = pair_site.shape[0]
    classes = kernel_table.shape[0]
    depth = NSC * z_count

    def exchange(array, axis):
        return lax.all_to_all(array, axis, split_axis=0, concat_axis=0, tiled=True)

    lists = jnp.concatenate([z_sites, pair_site, pair_combo[:, 0]]).reshape(1, -1, 128)
    lists = exchange(jnp.broadcast_to(lists, (slabs,) + lists.shape[1:]), "ta")

    idx_spec = pl.BlockSpec((1,) + lists.shape[1:], lambda t: (t, 0, 0))
    props_spec = pl.BlockSpec((1, rows, site_count), lambda t: (0, 0, t))
    z_rows = pl.pallas_call(
        z_gather_kernel,
        grid=(slabs,),
        in_specs=[idx_spec, props_spec],
        out_specs=pl.BlockSpec((1, 24, depth), lambda t: (t, 0, 0)),
        out_shape=jax.ShapeDtypeStruct((slabs, 24, depth), jnp.bfloat16),
        compiler_params=params(),
        cost_estimate=pl.CostEstimate(
            flops=2 * rows * site_count * z_count * slabs, bytes_accessed=15_000_000, transcendentals=0
        ),
        name="z_gather",
    )(lists, propagators)
    z_rows = exchange(z_rows, "ta")

    partner = pl.pallas_call(
        pair_gather_kernel,
        grid=(slabs,),
        in_specs=[idx_spec, props_spec],
        out_specs=pl.BlockSpec((rows, pair_count), lambda t: (0, t)),
        out_shape=jax.ShapeDtypeStruct((rows, slabs * pair_count), jnp.bfloat16),
        compiler_params=params(),
        cost_estimate=pl.CostEstimate(
            flops=2 * rows * site_count * pair_count * slabs, bytes_accessed=15_000_000, transcendentals=0
        ),
        name="pair_gather",
    )(lists, propagators)
    combo_ids = lists[:, 8:12, :].reshape(slabs, 1, pair_count)
    key = jnp.where(combo_ids // 16 % 16 == me, combo_ids // 256 * 16 + combo_ids % 16, -1)

    one_hot = (
        z_class[None, :] == jnp.arange(kernel_table.shape[1], dtype=jnp.int32)[:, None]
    ).astype(jnp.float32)
    weights = jnp.dot(kernel_table, one_hot, precision=lax.Precision.HIGHEST)

    per_step = 2
    sums = pl.pallas_call(
        combo_kernel,
        grid=(NSC // per_step,),
        in_specs=[
            pl.BlockSpec((slabs, 24, per_step * z_count), lambda l: (0, 0, l)),
            pl.BlockSpec((classes, per_step * z_count), lambda l: (0, 0)),
        ],
        out_specs=pl.BlockSpec((slabs, classes * 40, 128), lambda l: (0, 0, 0)),
        out_shape=jax.ShapeDtypeStruct((slabs, classes * 40, 128), jnp.float32),
        scratch_shapes=[pltpu.VMEM((classes, slabs * 24, slabs * 24), jnp.float32)],
        compiler_params=params(),
        cost_estimate=pl.CostEstimate(
            flops=2 * classes * 384 * 384 * depth, bytes_accessed=6_000_000, transcendentals=0
        ),
        name="combo_sums",
    )(z_rows, jnp.tile(weights, (1, per_step)))

    sums = jnp.sum(exchange(sums, "ta"), axis=0)
    sums = exchange(jnp.broadcast_to(sums[None], (blocks,) + sums.shape), "sa")

    group = 2
    found = pl.pallas_call(
        amplitude_kernel,
        grid=(slabs // group,),
        in_specs=[
            pl.BlockSpec(sums.shape, lambda t: (0, 0, 0)),
            pl.BlockSpec((1024, 64), lambda t: (0, 0)),
            pl.BlockSpec((320, 768), lambda t: (0, 0)),
            pl.BlockSpec((group, 1, pair_count), lambda t: (t, 0, 0)),
            pl.BlockSpec((rows, group * pair_count), lambda t: (0, t)),
        ],
        out_specs=pl.BlockSpec((group, 2, pair_count), lambda t: (t, 0, 0)),
        out_shape=jax.ShapeDtypeStruct((slabs, 2, pair_count), jnp.float32),
        scratch_shapes=[pltpu.VMEM((256, 288), jnp.bfloat16)],
        compiler_params=params(),
        name="amplitudes",
    )(
        sums,
        jnp.asarray(fold_matrix(), jnp.bfloat16),
        jnp.asarray(spread_matrix(), jnp.bfloat16),
        key,
        partner,
    )
    return jnp.sum(exchange(found, "ta"), axis=0)


def solution(mesh):
    placed = (
        P("ta", None, "sa"),
        P(("ta", "sa")),
        P(("ta", "sa")),
        P(),
        P(("ta", "sa"), None),
        P(("ta", "sa")),
    )
    return jax.shard_map(
        local, mesh=mesh, in_specs=placed, out_specs=P(None, ("ta", "sa")), check_vma=False
    )
```

time: 1020 us -> 177 us (0.17); the launches traced: 1010 us -> 176 us
  local copies, waits for them, and re-layouts: 328 us -> 3.23 us
  other arithmetic: 311 us -> 2.49 us
  waiting for transfers between devices: 264 us -> 72.6 us
  matrix products: 66.6 us -> 0.14 us
  Pallas kernels: 0 us -> 57.5 us
  blocking collectives: 0 us -> 23.3 us
  between operations: 14.1 us -> 0.03 us
    unnamed x1 -> x0, other arithmetic: 268 us -> none
    unnamed x2 -> x0, waiting for transfers between devices: 149 us -> none
    unnamed x22 -> x8, local copies, waits for them, and re-layouts: 110 us -> 1.48 us
    dot_general x1 -> x0, matrix products: 66.4 us -> none  [site_sums(): product = jnp.dot(weighted, extended, preferred_element_type=jnp.float32)]
    pallas_call x0 -> x4, Pallas kernels: none -> 57.5 us  [the longest x1 18.3 us: local(): pl.pallas_call(combo_kernel, grid=(NSC // per_step,), in_specs=[pl.BlockS...]
    all_to_all x3, waiting for transfers between devices: 115 us -> 72.6 us  [exchange(): return lax.all_to_all(array, axis, split_axis=0, concat_axis=0, tiled=True)]
    all_to_all x3 -> x0, local copies, waits for them, and re-layouts: 40.5 us -> none  [the longest x1 36.9 us: local(): lax.all_to_all(propagators, 'ta', split_axis=2, concat_axis=0, tiled=True)]
    transpose x4 -> x0, local copies, waits for them, and re-layouts: 39.5 us -> none  [the longest x3 29.8 us: trace_pair(): jnp.swapaxes(prop_mat.astype(jnp.float32).reshape(-1, 2, 12, 12), 2, 3)]
  transfers between devices with their start and end apart: 4 -> 3, of which waited for: 3 -> 2; matrix products, arithmetic and copies ran while one was open for 20% -> 2% of each run, Pallas kernels for 0% -> 9%
where the time goes in v1:
time: 177 us; the launch traced here: 176 us
  waiting for transfers between devices  72.6 us (41%)
  Pallas kernels  57.5 us (32%)
  blocking collectives  23.3 us (13%)
  starting transfers between devices  16.6 us (9%)
  local copies, waits for them, and re-layouts  3.23 us (2%)
  other arithmetic  2.49 us (1%)
    all_to_all x3, waiting for transfers between devices, exchange(): return lax.all_to_all(array, axis, split_axis=0, concat_axis=0, tiled=True)  72.6 us
    all_to_all x2, blocking collectives, exchange(): return lax.all_to_all(array, axis, split_axis=0, concat_axis=0, tiled=True)  23.3 us
    pallas_call x1, Pallas kernels, local(): pl.pallas_call(combo_kernel, grid=(NSC // per_step,), in_specs=[pl.BlockS...  18.3 us
    all_to_all x3, starting transfers between devices, exchange(): return lax.all_to_all(array, axis, split_axis=0, concat_axis=0, tiled=True)  16.6 us
    pallas_call x1, Pallas kernels, local(): pl.pallas_call(pair_gather_kernel, grid=(slabs,), in_specs=[idx_spec, pro...  15.1 us
    pallas_call x1, Pallas kernels, local(): pl.pallas_call(z_gather_kernel, grid=(slabs,), in_specs=[idx_spec, props_...  15 us
    pallas_call x1, Pallas kernels, local(): pl.pallas_call(amplitude_kernel, grid=(slabs // group,), in_specs=[pl.Blo...  9.08 us
  transfers between devices with their start and end apart: 3, of which 2 were waited for; matrix products, arithmetic and copies ran while one was open for 2% of the time, Pallas kernels for 9%

profile of v1, /device:TPU:1, one launch (start us, length us, event | category | flops | bytes accessed | tf_op | source)
XLA Modules:
  0.0 175.8 jit_solution(2786585457752412801)
XLA Ops:
  0.0 0.0 copy-start
  0.0 0.7 pad_add_fusion
  0.8 13.0 %all_to_all.25.idx_ref = s32[16,12,128]{2,1,0:T(8,128)} all-to-all(s32[16,12,128]{2,1,0:T(8,128)S(1)} %broadcast_in_dim.6), channel_id=1, replica_groups=mesh['ta'=16,'sa'=8] {'ta'}, dimensions={0} | all-to-all | bytes 196608 | tf_op jit(solution)/shard_map/all_to_all | solution.py:191
  13.7 15.0 %z_gather.1 = bf16[16,24,6144]{2,1,0:T(8,128)(2,1)} custom-call(s32[16,12,128]{2,1,0:T(8,128)} %all_to_all.25.idx_ref, bf16[1,288,16384]{2,1,0:T(8,128)(2,1)} %props_ref.3), custom_call_target="tpu_custom_call" | custom-call | flops 4831838208 | bytes 15000000 | tf_op jit(solution)/shard_map/z_gather/pallas_call | solution.py:198
  28.7 0.0 copy-start.2
  28.7 5.1 %all-to-all-start.1 = ((bf16[16,24,6144]{2,1,0:T(8,128)(2,1)}), bf16[16,24,6144]{2,1,0:T(8,128)(2,1)}, u32[]{:S(2)}, u32[]{:S(2)}) async-start(bf16[16,24,6144]{2,1,0:T(8,128)(2,1)} %z_gather.1), calls=%async_computation.1 | async-start | bytes 9437184 | tf_op jit(solution)/shard_map/all_to_all | solution.py:191
  33.8 0.0 copy-done
  33.8 0.0 copy-done.2
  33.8 0.1 convolution_bitcast_fusion
  34.0 0.6 copy.9
  34.6 54.6 %all-to-all-done.1.x_ref = bf16[16,24,6144]{2,1,0:T(8,128)(2,1)} async-done(((bf16[16,24,6144]{2,1,0:T(8,128)(2,1)}), bf16[16,24,6144]{2,1,0:T(8,128)(2,1)}, u32[]{:S(2)}, u32[]{:S(2)}) %all-to-all-start.1) | async-done | bytes 4718624 | tf_op jit(solution)/shard_map/all_to_all | solution.py:191
  89.2 18.3 %combo_sums.1 = f32[16,160,128]{2,1,0:T(8,128)} custom-call(bf16[16,24,6144]{2,1,0:T(8,128)(2,1)} %all-to-all-done.1.x_ref, f32[4,1024]{1,0:T(4,128)} %bitcast.11), custom_call_target="tpu_custom_call" | custom-call | flops 7247757312 | bytes 6000000 | tf_op jit(solution)/shard_map/combo_sums/pallas_call | solution.py:233
  107.5 4.3 %all-to-all-start.2 = ((f32[16,160,128]{2,1,0:T(8,128)}), f32[16,160,128]{2,1,0:T(8,128)S(1)}, u32[]{:S(2)}, u32[]{:S(2)}) async-start(f32[16,160,128]{2,1,0:T(8,128)} %combo_sums.1), calls=%async_computation.2 | async-start | bytes 2621440 | tf_op jit(solution)/shard_map/all_to_all | solution.py:191
  111.9 0.8 slice.4
  112.7 17.9 %all-to-all-done.2 = f32[16,160,128]{2,1,0:T(8,128)S(1)} async-done(((f32[16,160,128]{2,1,0:T(8,128)}), f32[16,160,128]{2,1,0:T(8,128)S(1)}, u32[]{:S(2)}, u32[]{:S(2)}) %all-to-all-start.2) | async-done | bytes 1310752 | tf_op jit(solution)/shard_map/all_to_all | solution.py:191
  130.6 0.1 reduce_sum.18
  130.7 0.9 broadcast_in_dim.7
  131.6 7.2 %all-to-all-start.3 = ((f32[8,160,128]{2,1,0:T(8,128)}), f32[8,160,128]{2,1,0:T(8,128)S(1)}, u32[]{:S(2)}, u32[]{:S(2)}) async-start(f32[8,160,128]{2,1,0:T(8,128)} %broadcast_in_dim.7), calls=%async_computation.3 | async-start | bytes 1310720 | tf_op jit(solution)/shard_map/all_to_all | solution.py:191
  138.8 1.1 compare_select_fusion.2.key_ref
  139.9 15.1 %pair_gather.1.partner_ref = bf16[288,8192]{1,0:T(8,128)(2,1)} custom-call(s32[16,12,128]{2,1,0:T(8,128)} %all_to_all.25.idx_ref, bf16[1,288,16384]{2,1,0:T(8,128)(2,1)} %props_ref.3), custom_call_target="tpu_custom_call" | custom-call | flops 4831838208 | bytes 15000000 | tf_op jit(solution)/shard_map/pair_gather/pallas_call | solution.py:212
  155.0 0.0 all-to-all-done.3.sums_ref
  155.0 0.0 copy-start.1
  155.0 0.9 copy-done.1
  155.8 9.1 %amplitudes.1 = f32[16,2,512]{2,1,0:T(2,128)} custom-call(f32[8,160,128]{2,1,0:T(8,128)} %copy-done.1, bf16[1024,64]{1,0:T(8,128)(2,1)} %constant.58.clone.fold_ref, bf16[320,768]{1,0:T(8,128)(2,1)} %constant.59.clone.spread_ref, s32[16,1,512]{2,1,0:T(1,128)} %compare_select_fusion.2.key_ref, bf16[288,8192]{1,0:T(8,128)(2,1)} %pair_gather.1.partner_ref), custom_call_target="tpu_custom_call" | custom-call | tf_op jit(solution)/shard_map/amplitudes/pallas_call | solution.py:254
  164.9 10.3 %all_to_all.26 = f32[16,2,512]{2,1,0:T(2,128)S(1)} all-to-all(f32[16,2,512]{2,1,0:T(2,128)} %amplitudes.1), channel_id=1, replica_groups=mesh['ta'=16,'sa'=8] {'ta'}, dimensions={0} | all-to-all | bytes 131072 | tf_op jit(solution)/shard_map/all_to_all | solution.py:191
  175.2 0.6 reduce_sum.19
  (2 shorter events, 0.0 us)
Async XLA Ops:
  0.0 33.8 %copy-start = (f32[4,32]{1,0:T(4,128)S(1)}, f32[4,32]{1,0:T(4,128)}, u32[]{:S(2)}) copy-start(f32[4,32]{1,0:T(4,128)} %param.11) | copy-start | bytes 1540
  28.7 5.1 %copy-start.2 = (s32[512]{0:T(512)S(1)}, s32[512]{0:T(512)}, u32[]{:S(2)}) copy-start(s32[512]{0:T(512)} %param.10) | copy-start | bytes 6148
  28.7 60.5 %all-to-all-start.1 = ((bf16[16,24,6144]{2,1,0:T(8,128)(2,1)}), bf16[16,24,6144]{2,1,0:T(8,128)(2,1)}, u32[]{:S(2)}, u32[]{:S(2)}) async-start(bf16[16,24,6144]{2,1,0:T(8,128)(2,1)} %z_gather.1), calls=%async_computation.1 | async-start | bytes 9437184 | tf_op jit(solution)/shard_map/all_to_all | solution.py:191
  107.5 23.1 %all-to-all-start.2 = ((f32[16,160,128]{2,1,0:T(8,128)}), f32[16,160,128]{2,1,0:T(8,128)S(1)}, u32[]{:S(2)}, u32[]{:S(2)}) async-start(f32[16,160,128]{2,1,0:T(8,128)} %combo_sums.1), calls=%async_computation.2 | async-start | bytes 2621440 | tf_op jit(solution)/shard_map/all_to_all | solution.py:191
  131.6 23.4 %all-to-all-start.3 = ((f32[8,160,128]{2,1,0:T(8,128)}), f32[8,160,128]{2,1,0:T(8,128)S(1)}, u32[]{:S(2)}, u32[]{:S(2)}) async-start(f32[8,160,128]{2,1,0:T(8,128)} %broadcast_in_dim.7), calls=%async_computation.3 | async-start | bytes 1310720 | tf_op jit(solution)/shard_map/all_to_all | solution.py:191
  155.0 0.9 copy-start.1

commit v2 on v0

v2 whole, which is shorter than its diff:
```python
import functools

import jax
import jax.numpy as jnp
import numpy as np
from jax import lax
from jax.experimental import pallas as pl
from jax.experimental.pallas import tpu as pltpu
from jax.sharding import PartitionSpec as P

NSC = 12

def one_hot_columns(idx_row, count):
    rows = lax.broadcasted_iota(jnp.int32, (count, idx_row.shape[1]), 0)
    return jnp.where(rows == idx_row, 1.0, 0.0).astype(jnp.bfloat16)


def z_gather_kernel(idx_ref, props_ref, after_ref, out_ref, held_ref, sems):
    slabs = out_ref.shape[0]
    count = out_ref.shape[2] // NSC

    def send(t):
        return pltpu.make_async_copy(held_ref.at[t], out_ref.at[t], sems.at[t])

    sites = props_ref.shape[2] // slabs
    half = NSC * NSC

    def pair_of_slabs(u, carry):
        for t in (2 * u, 2 * u + 1):
            idx = idx_ref[t]
            hot = jnp.concatenate([one_hot_columns(idx[r : r + 1, :], sites) for r in range(4)], axis=1)
            block = props_ref[0, :, pl.ds(pl.multiple_of(t * sites, sites), sites)]
            picked = jnp.dot(block, hot, preferred_element_type=jnp.float32)
            for l in range(NSC):
                re, im = l * NSC, half + l * NSC
                held_ref[t, :, l * count : (l + 1) * count] = jnp.concatenate(
                    [
                        picked[re : re + 8],
                        picked[im : im + 8],
                        picked[re + 8 : re + 12],
                        picked[im + 8 : im + 12],
                    ],
                    axis=0,
                ).astype(jnp.bfloat16)
            send(t).start()
        return carry

    lax.fori_loop(0, slabs // 2, pair_of_slabs, 0)
    for t in range(slabs):
        send(t).wait()


def pair_pick_kernel(me_ref, idx_ref, props_ref, out_ref):
    slabs = idx_ref.shape[0]
    sites = props_ref.shape[2] // slabs
    lax.fori_loop(0, slabs, functools.partial(pick_block, me_ref, idx_ref, props_ref, out_ref, sites), 0)


def pick_block(me_ref, idx_ref, props_ref, out_ref, sites, t, carry):
    idx = idx_ref[t]
    far = 1 << 20
    ids = lax.broadcasted_iota(jnp.int32, (64, 128), 0)
    lane = lax.broadcasted_iota(jnp.int32, (1, 128), 1)
    first = jnp.full((64, 128), far, jnp.int32)
    last = jnp.full((64, 128), -1, jnp.int32)
    for r in range(4):
        combo = idx[8 + r : 9 + r, :]
        key = jnp.where(combo // 16 % 16 == me_ref[0], combo // 256 * 16 + combo % 16, -1)
        code = (r * 128 + lane) * sites + idx[4 + r : 5 + r, :]
        mine = ids == key
        first = jnp.minimum(first, jnp.where(mine, code, far))
        last = jnp.maximum(last, jnp.where(mine, code, -1))
    first = jnp.min(first, axis=1, keepdims=True)
    last = jnp.max(last, axis=1, keepdims=True)
    found = jnp.concatenate([first, last], axis=0)
    place = jnp.where((found >= 0) & (found < far), found % sites, -1)
    hot = jnp.where(
        lax.broadcasted_iota(jnp.int32, (128, sites), 1) == place, 1.0, 0.0
    ).astype(jnp.bfloat16)
    block = props_ref[0, :, pl.ds(pl.multiple_of(t * sites, sites), sites)]
    out_ref[:, pl.ds(pl.multiple_of(t * 128, 128), 128)] = lax.dot_general(
        block, hot, (((1,), (1,)), ((), ())), preferred_element_type=jnp.float32
    ).astype(jnp.bfloat16)
    return carry


def combo_kernel(x_ref, w_ref, after_ref, out_ref, held_ref, acc_ref, sems):
    sources, _, lanes = x_ref.shape
    classes, count = w_ref.shape
    per = 4
    depth = per * count
    n = sources * 8

    def piece(s):
        at = pl.ds(pl.multiple_of(s * depth, depth), depth)
        return pltpu.make_async_copy(x_ref.at[:, :, at], held_ref.at[s], sems.at[s])

    for s in range(lanes // depth):
        piece(s).start()

    def chunk(s, carry):
        piece(s).wait()
        wide = held_ref[s].astype(jnp.float32)
        rows = jnp.concatenate(
            [wide[:, 8 * t : 8 * t + 8, :].reshape(n, depth) for t in range(3)], axis=0
        )
        right = rows.astype(jnp.bfloat16)
        left = jnp.concatenate(
            [
                (rows * jnp.concatenate([w_ref[c : c + 1, :]] * per, axis=1)).astype(jnp.bfloat16)
                for c in range(classes)
            ],
            axis=0,
        )
        part = lax.dot_general(
            left, right, (((1,), (1,)), ((), ())), preferred_element_type=jnp.float32
        )

        @pl.when(s == 0)
        def _():
            acc_ref[...] = part

        @pl.when(s > 0)
        def _():
            acc_ref[...] += part

        return carry

    lax.fori_loop(0, lanes // depth, chunk, 0)

    low_row = lax.broadcasted_iota(jnp.int32, (n, n), 0) % 8 < 4
    low_lane = lax.broadcasted_iota(jnp.int32, (n, n), 1) % 8 < 4

    def swap_rows(m):
        return pltpu.roll(m.reshape(sources, 8, n), 4, 1).reshape(n, n)

    def swap_lanes(m):
        return jnp.where(low_lane, pltpu.roll(m, n - 4, 1), pltpu.roll(m, 4, 1))

    for c in range(classes):

        def blk(a_tile, b_tile):
            at = c * 3 * n + n * b_tile
            return acc_ref[at : at + n, n * a_tile : n * a_tile + n]

        re = blk(0, 0) + blk(1, 1)
        im = blk(1, 0) - blk(0, 1)
        a, b = blk(0, 2), swap_rows(blk(1, 2))
        wide_col = jnp.where(low_row, a + b, b - a)
        a, b = blk(2, 0), swap_lanes(blk(2, 1))
        tall_row = jnp.where(low_lane, a + b, a - b)
        a = blk(2, 2)
        b = swap_lanes(swap_rows(a))
        corner = jnp.where(low_row, jnp.where(low_lane, a + b, a - b), 0.0)
        for k, m in enumerate((re, im, wide_col, tall_row, corner)):
            at = (c * 5 + k) * 8
            out_ref[:, at : at + 8, :] = m.T.reshape(sources, 8, n)


def spread_matrix():
    out = np.zeros((5, 8, 8, 768), np.float32)

    def put(k, r, q, j, i, imag):
        at = j * NSC + i
        half = NSC * NSC
        if imag:
            out[k, r, q, half + at] = -1.0
            out[k, r, q, 384 + at] = 1.0
        else:
            out[k, r, q, at] = 1.0
            out[k, r, q, 384 + half + at] = 1.0

    for r in range(8):
        for q in range(8):
            put(0, r, q, r, q, False)
            put(1, r, q, r, q, True)
            put(2, r, q, r, 8 + q % 4, q >= 4)
            put(3, r, q, 8 + r % 4, q, r >= 4)
            if q < 4:
                put(4, r, q, 8 + r % 4, 8 + q, r >= 4)
    return out.reshape(320, 768)


def fold_matrix():
    r = np.arange(1024)[:, None] // 128
    q = np.arange(1024)[:, None] % 8
    return (np.arange(64)[None, :] == r * 8 + q).astype(np.float32)


def amplitude_kernel(sums_ref, fold_ref, spread_ref, partner_ref, out_ref):
    classes, sources = 4, 16
    combos = classes * sources
    sums = jnp.sum(sums_ref[...], axis=0)
    own = (
        lax.broadcasted_iota(jnp.int32, (sources, 128), 1) // 8
        == lax.broadcasted_iota(jnp.int32, (sources, 128), 0)
    )
    total = jnp.zeros((2 * combos, 768), jnp.float32)
    for k in range(5):
        tall = []
        for c in range(classes):
            at = (c * 5 + k) * 8
            tall.append(
                jnp.concatenate(
                    [
                        jnp.where(own, jnp.broadcast_to(sums[at + r : at + r + 1, :], (sources, 128)), 0.0)
                        for r in range(8)
                    ],
                    axis=1,
                )
            )
        tall = jnp.concatenate(tall, axis=0)
        high = tall.astype(jnp.bfloat16)
        low = (tall - high.astype(jnp.float32)).astype(jnp.bfloat16)
        both = jnp.concatenate([high, low], axis=0)
        folded = jnp.dot(both, fold_ref[...], preferred_element_type=jnp.float32)
        total += jnp.dot(
            folded.astype(jnp.bfloat16),
            spread_ref[64 * k : 64 * k + 64, :],
            preferred_element_type=jnp.float32,
        )
    rows = partner_ref.shape[0]
    probe = jnp.concatenate([total[:, 0:rows], total[:, 384 : 384 + rows]], axis=0).astype(jnp.bfloat16)
    traces = jnp.dot(probe, partner_ref[...], preferred_element_type=jnp.float32)
    mine = (
        lax.broadcasted_iota(jnp.int32, (combos, 128), 1) % combos
        == lax.broadcasted_iota(jnp.int32, (combos, 128), 0)
    )
    for t in range(out_ref.shape[0]):
        lanes = slice(t * 128, t * 128 + 128)
        for part in range(2):
            at = part * 2 * combos
            value = traces[at : at + combos, lanes] + traces[at + combos : at + 2 * combos, lanes]
            out_ref[t, part : part + 1, :] = jnp.sum(jnp.where(mine, value, 0.0), axis=0, keepdims=True)


def home_kernel(back_ref, slot_ref, source_ref, out_ref):
    sources, _, slots = back_ref.shape
    pairs = slot_ref.shape[1]
    rest = jnp.concatenate([back_ref[:, 0, :], back_ref[:, 1, :]], axis=0)
    parts = []
    for _ in range(3):
        part = rest.astype(jnp.bfloat16)
        rest = rest - part.astype(jnp.float32)
        parts.append(part)
    hot = jnp.where(
        lax.broadcasted_iota(jnp.int32, (slots, pairs), 0) == slot_ref[...], 1.0, 0.0
    ).astype(jnp.bfloat16)
    spread = jnp.dot(jnp.concatenate(parts, axis=0), hot, preferred_element_type=jnp.float32)
    n = 2 * sources
    value = (spread[0:n] + spread[n : 2 * n]) + spread[2 * n : 3 * n]
    mine = lax.broadcasted_iota(jnp.int32, (sources, pairs), 0) == source_ref[...]
    for part in range(2):
        out_ref[part : part + 1, :] = jnp.sum(
            jnp.where(mine, value[part * sources : (part + 1) * sources], 0.0), axis=0, keepdims=True
        )


def params(mebibytes):
    return pltpu.CompilerParams(vmem_limit_bytes=mebibytes * 1024 * 1024)


IN_VMEM = pl.BlockSpec(memory_space=pltpu.VMEM)


def local(propagators, z_sites, z_class, kernel_table, pair_combo, pair_site):
    slabs = lax.axis_size("ta")
    blocks = lax.axis_size("sa")
    me = lax.axis_index("ta")
    rows = propagators.shape[1]
    site_count = propagators.shape[2] // slabs
    z_count = z_sites.shape[0]
    pair_count = pair_site.shape[0]
    classes = kernel_table.shape[0]
    depth = NSC * z_count

    def exchange(array, axis):
        return lax.all_to_all(array, axis, split_axis=0, concat_axis=0, tiled=True)

    lists = jnp.concatenate([z_sites, pair_site, pair_combo[:, 0]]).reshape(1, -1, 128)
    lists = exchange(jnp.broadcast_to(lists, (slabs,) + lists.shape[1:]), "ta")

    one_hot = (
        z_class[None, :] == jnp.arange(kernel_table.shape[1], dtype=jnp.int32)[:, None]
    ).astype(jnp.float32)
    weights = jnp.dot(kernel_table, one_hot, precision=lax.Precision.HIGHEST)

    z_rows = pl.pallas_call(
        z_gather_kernel,
        in_specs=[IN_VMEM, IN_VMEM, pl.BlockSpec(memory_space=pl.ANY)],
        out_specs=pl.BlockSpec(memory_space=pl.ANY),
        out_shape=jax.ShapeDtypeStruct((slabs, 24, depth), jnp.bfloat16),
        scratch_shapes=[
            pltpu.VMEM((slabs, 24, depth), jnp.bfloat16),
            pltpu.SemaphoreType.DMA((slabs,)),
        ],
        compiler_params=params(52),
        cost_estimate=pl.CostEstimate(
            flops=2 * rows * site_count * z_count * slabs, bytes_accessed=15_000_000, transcendentals=0
        ),
        name="z_gather",
    )(lists, propagators, weights)
    z_rows = exchange(z_rows, "ta")

    slots = 128
    partner = pl.pallas_call(
        pair_pick_kernel,
        in_specs=[pl.BlockSpec(memory_space=pltpu.SMEM), IN_VMEM, IN_VMEM],
        out_specs=IN_VMEM,
        out_shape=jax.ShapeDtypeStruct((rows, slabs * slots), jnp.bfloat16),
        compiler_params=params(16),
        cost_estimate=pl.CostEstimate(
            flops=2 * rows * site_count * slots * slabs, bytes_accessed=11_000_000, transcendentals=0
        ),
        name="pair_pick",
    )(me.astype(jnp.int32).reshape(1), lists, propagators)

    combo_ids = pair_combo[:, 0]
    counter = jnp.arange(pair_count, dtype=jnp.int32)
    second = jnp.any(
        (combo_ids[:, None] == combo_ids[None, :]) & (counter[None, :] < counter[:, None]), axis=1
    )
    slot = combo_ids // 256 * 16 + combo_ids % 16 + jnp.where(second, 64, 0)
    source = combo_ids // 16 % 16

    sums = pl.pallas_call(
        combo_kernel,
        in_specs=[pl.BlockSpec(memory_space=pl.ANY), IN_VMEM, pl.BlockSpec(memory_space=pl.ANY)],
        out_specs=IN_VMEM,
        out_shape=jax.ShapeDtypeStruct((slabs, classes * 40, 128), jnp.float32),
        scratch_shapes=[
            pltpu.VMEM((3, slabs, 24, depth // 3), jnp.bfloat16),
            pltpu.VMEM((classes * slabs * 24, slabs * 24), jnp.float32),
            pltpu.SemaphoreType.DMA((3,)),
        ],
        compiler_params=params(32),
        cost_estimate=pl.CostEstimate(
            flops=2 * classes * 384 * 384 * depth, bytes_accessed=6_000_000, transcendentals=0
        ),
        name="combo_sums",
    )(z_rows, weights, partner)

    sums = jnp.sum(exchange(sums, "ta"), axis=0)
    sums = exchange(jnp.broadcast_to(sums[None], (blocks,) + sums.shape), "sa")

    found = pl.pallas_call(
        amplitude_kernel,
        in_specs=[IN_VMEM] * 4,
        out_specs=IN_VMEM,
        out_shape=jax.ShapeDtypeStruct((slabs, 2, slots), jnp.float32),
        compiler_params=params(32),
        name="amplitudes",
    )(
        sums,
        jnp.asarray(fold_matrix(), jnp.bfloat16),
        jnp.asarray(spread_matrix(), jnp.bfloat16),
        partner,
    )
    back = exchange(found, "ta")
    return pl.pallas_call(
        home_kernel,
        in_specs=[IN_VMEM] * 3,
        out_specs=IN_VMEM,
        out_shape=jax.ShapeDtypeStruct((2, pair_count), jnp.float32),
        compiler_params=params(16),
        name="home",
    )(back, slot.reshape(1, -1), source.reshape(1, -1))


def solution(mesh):
    placed = (
        P("ta", None, "sa"),
        P(("ta", "sa")),
        P(("ta", "sa")),
        P(),
        P(("ta", "sa"), None),
        P(("ta", "sa")),
    )
    return jax.shard_map(
        local, mesh=mesh, in_specs=placed, out_specs=P(None, ("ta", "sa")), check_vma=False
    )
```

time: 1020 us -> 156 us (0.15); the launches traced: 1010 us -> 156 us
  local copies, waits for them, and re-layouts: 328 us -> 5.24 us
  other arithmetic: 311 us -> 1.09 us
  waiting for transfers between devices: 264 us -> 62.9 us
  matrix products: 66.6 us -> 0.82 us
  Pallas kernels: 0 us -> 37.4 us
  blocking collectives: 0 us -> 22.2 us
  between operations: 14.1 us -> 0.08 us
    unnamed x1 -> x0, other arithmetic: 268 us -> none
    unnamed x2 -> x0, waiting for transfers between devices: 149 us -> none
    unnamed x22 -> x10, local copies, waits for them, and re-layouts: 110 us -> 3.7 us
    dot_general x1 -> x0, matrix products: 66.4 us -> none  [site_sums(): product = jnp.dot(weighted, extended, preferred_element_type=jnp.float32)]
    all_to_all x3 -> x4, waiting for transfers between devices: 115 us -> 62.9 us  [exchange(): return lax.all_to_all(array, axis, split_axis=0, concat_axis=0, tiled=True)]
    all_to_all x3 -> x0, local copies, waits for them, and re-layouts: 40.5 us -> none  [the longest x1 36.9 us: local(): lax.all_to_all(propagators, 'ta', split_axis=2, concat_axis=0, tiled=True)]
    transpose x4 -> x0, local copies, waits for them, and re-layouts: 39.5 us -> none  [the longest x3 29.8 us: trace_pair(): jnp.swapaxes(prop_mat.astype(jnp.float32).reshape(-1, 2, 12, 12), 2, 3)]
    pallas_call x0 -> x5, Pallas kernels: none -> 37.4 us  [the longest x1 13.2 us: local(): pl.pallas_call(combo_kernel, in_specs=[pl.BlockSpec(memory_space=pl.ANY),...]
  transfers between devices with their start and end apart: 4 -> 4, of which waited for: 3 -> 4; matrix products, arithmetic and copies ran while one was open for 20% -> 1% of each run, Pallas kernels for 0% -> 6%
where the time goes in v2:
time: 156 us
  waiting for transfers between devices  62.9 us (40%)
  Pallas kernels  37.4 us (24%)
  starting transfers between devices  25.8 us (17%)
  blocking collectives  22.2 us (14%)
  local copies, waits for them, and re-layouts  5.24 us (3%)
    all_to_all x4, waiting for transfers between devices, exchange(): return lax.all_to_all(array, axis, split_axis=0, concat_axis=0, tiled=True)  62.9 us
    all_to_all x4, starting transfers between devices, exchange(): return lax.all_to_all(array, axis, split_axis=0, concat_axis=0, tiled=True)  25.8 us
    all_to_all x1, blocking collectives, exchange(): return lax.all_to_all(array, axis, split_axis=0, concat_axis=0, tiled=True)  22.2 us
    pallas_call x1, Pallas kernels, local(): pl.pallas_call(combo_kernel, in_specs=[pl.BlockSpec(memory_space=pl.ANY),...  13.2 us
    pallas_call x1, Pallas kernels, local(): pl.pallas_call(z_gather_kernel, in_specs=[IN_VMEM, IN_VMEM, pl.BlockSpec(...  11.6 us
    pallas_call x1, Pallas kernels, local(): pl.pallas_call(pair_pick_kernel, in_specs=[pl.BlockSpec(memory_space=pltp...  9.38 us
    unnamed x10, local copies, waits for them, and re-layouts  3.7 us
  transfers between devices with their start and end apart: 4, of which 4 were waited for; matrix products, arithmetic and copies ran while one was open for 1% of the time, Pallas kernels for 6%

profile of v2, /device:TPU:1, one launch (start us, length us, event | category | flops | bytes accessed | tf_op | source)
XLA Modules:
  0.0 155.5 jit_solution(13590422325405620589)
XLA Ops:
  0.0 0.0 copy-start
  0.0 0.7 pad_add_fusion
  0.7 0.7 broadcast_in_dim.8
  1.4 6.9 %all-to-all-start = ((s32[16,12,128]{2,1,0:T(8,128)}), s32[16,12,128]{2,1,0:T(8,128)S(1)}, u32[]{:S(2)}, u32[]{:S(2)}) async-start(s32[16,12,128]{2,1,0:T(8,128)} %broadcast_in_dim.8), calls=%async_computation | async-start | bytes 262144 | tf_op jit(solution)/shard_map/all_to_all | solution.py:278
  8.3 0.0 copy-done
  8.3 0.8 convolution_bitcast_fusion.after_ref.w_ref
  9.1 5.3 %all-to-all-done.idx_ref = s32[16,12,128]{2,1,0:T(8,128)S(1)} async-done(((s32[16,12,128]{2,1,0:T(8,128)}), s32[16,12,128]{2,1,0:T(8,128)S(1)}, u32[]{:S(2)}, u32[]{:S(2)}) %all-to-all-start) | async-done | bytes 98336 | tf_op jit(solution)/shard_map/all_to_all | solution.py:278
  14.5 11.6 %z_gather.1 = bf16[16,24,6144]{2,1,0:T(8,128)(2,1)} custom-call(s32[16,12,128]{2,1,0:T(8,128)S(1)} %all-to-all-done.idx_ref, bf16[1,288,16384]{2,1,0:T(8,128)(2,1)} %props_ref.3, f32[4,512]{1,0:T(4,128)S(1)} %convolution_bitcast_fusion.after_ref.w_ref), custom_call_target="tpu_custom_call" | custom-call | flops 4831838208 | bytes 15000000 | tf_op jit(solution)/shard_map/z_gather/pallas_call | solution.py:288
  26.0 5.0 %all-to-all-start.1 = ((bf16[16,24,6144]{2,1,0:T(8,128)(2,1)}), bf16[16,24,6144]{2,1,0:T(8,128)(2,1)}, u32[]{:S(2)}, u32[]{:S(2)}) async-start(bf16[16,24,6144]{2,1,0:T(8,128)(2,1)} %z_gather.1), calls=%async_computation.1 | async-start | bytes 9437184 | tf_op jit(solution)/shard_map/all_to_all | solution.py:278
  31.0 0.0 copy-start.1
  31.0 3.7 %copy-done.1 = bf16[1,288,16384]{2,1,0:T(8,128)(2,1)S(1)} copy-done((bf16[1,288,16384]{2,1,0:T(8,128)(2,1)S(1)}, bf16[1,288,16384]{2,1,0:T(8,128)(2,1)}, u32[]{:S(2)}) %copy-start.1) | copy-done | bytes 9437208
  34.7 9.4 %pair_pick.1.after_ref.partner_ref = bf16[288,2048]{1,0:T(8,128)(2,1)S(1)} custom-call(s32[1]{0:T(128)} %bitcast.4.me_ref, s32[16,12,128]{2,1,0:T(8,128)S(1)} %all-to-all-done.idx_ref, bf16[1,288,16384]{2,1,0:T(8,128)(2,1)S(1)} %copy-done.1), custom_call_target="tpu_custom_call" | custom-call | flops 1207959552 | bytes 11000000 | tf_op jit(solution)/shard_map/pair_pick/pallas_call | solution.py:306
  44.1 42.3 %all-to-all-done.1.x_ref = bf16[16,24,6144]{2,1,0:T(8,128)(2,1)} async-done(((bf16[16,24,6144]{2,1,0:T(8,128)(2,1)}), bf16[16,24,6144]{2,1,0:T(8,128)(2,1)}, u32[]{:S(2)}, u32[]{:S(2)}) %all-to-all-start.1) | async-done | bytes 4718624 | tf_op jit(solution)/shard_map/all_to_all | solution.py:278
  86.4 13.2 %combo_sums.1 = f32[16,160,128]{2,1,0:T(8,128)S(1)} custom-call(bf16[16,24,6144]{2,1,0:T(8,128)(2,1)} %all-to-all-done.1.x_ref, f32[4,512]{1,0:T(4,128)S(1)} %convolution_bitcast_fusion.after_ref.w_ref, bf16[288,2048]{1,0:T(8,128)(2,1)S(1)} %pair_pick.1.after_ref.partner_ref), custom_call_target="tpu_custom_call" | custom-call | flops 7247757312 | bytes 6000000 | tf_op jit(solution)/shard_map/combo_sums/pallas_call | solution.py:326
  99.6 0.0 copy-start.4
  99.6 0.0 copy-start.2
  99.6 0.0 copy-start.3
  99.6 22.2 %all_to_all.25 = f32[16,160,128]{2,1,0:T(8,128)S(1)} all-to-all(f32[16,160,128]{2,1,0:T(8,128)S(1)} %combo_sums.1), channel_id=1, replica_groups=mesh['ta'=16,'sa'=8] {'ta'}, dimensions={0} | all-to-all | bytes 2621440 | tf_op jit(solution)/shard_map/all_to_all | solution.py:278
  121.8 0.1 reduce_sum.9
  121.9 0.9 broadcast_in_dim.11
  122.7 7.2 %all-to-all-start.3 = ((f32[8,160,128]{2,1,0:T(8,128)}), f32[8,160,128]{2,1,0:T(8,128)S(1)}, u32[]{:S(2)}, u32[]{:S(2)}) async-start(f32[8,160,128]{2,1,0:T(8,128)} %broadcast_in_dim.11), calls=%async_computation.3 | async-start | bytes 1310720 | tf_op jit(solution)/shard_map/all_to_all | solution.py:278
  129.9 0.0 copy-done.4
  130.0 0.2 fusion.1
  130.2 9.4 %all-to-all-done.3.sums_ref = f32[8,160,128]{2,1,0:T(8,128)S(1)} async-done(((f32[8,160,128]{2,1,0:T(8,128)}), f32[8,160,128]{2,1,0:T(8,128)S(1)}, u32[]{:S(2)}, u32[]{:S(2)}) %all-to-all-start.3) | async-done | bytes 655392 | tf_op jit(solution)/shard_map/all_to_all | solution.py:278
  139.7 0.0 copy-done.2
  139.7 0.0 copy-done.3
  139.7 2.5 %amplitudes.1 = f32[16,2,128]{2,1,0:T(2,128)} custom-call(f32[8,160,128]{2,1,0:T(8,128)S(1)} %all-to-all-done.3.sums_ref, bf16[1024,64]{1,0:T(8,128)(2,1)S(1)} %copy-done.3, bf16[320,768]{1,0:T(8,128)(2,1)S(1)} %copy-done.2, bf16[288,2048]{1,0:T(8,128)(2,1)S(1)} %pair_pick.1.after_ref.partner_ref), custom_call_target="tpu_custom_call" | custom-call | tf_op jit(solution)/shard_map/amplitudes/pallas_call | solution.py:346
  142.2 6.8 %all-to-all-start.4 = ((f32[16,2,128]{2,1,0:T(2,128)}), f32[16,2,128]{2,1,0:T(2,128)S(1)}, u32[]{:S(2)}, u32[]{:S(2)}) async-start(f32[16,2,128]{2,1,0:T(2,128)} %amplitudes.1), calls=%async_computation.4 | async-start | bytes 32768 | tf_op jit(solution)/shard_map/all_to_all | solution.py:278
  149.0 5.8 %all-to-all-done.4.back_ref = f32[16,2,128]{2,1,0:T(2,128)S(1)} async-done(((f32[16,2,128]{2,1,0:T(2,128)}), f32[16,2,128]{2,1,0:T(2,128)S(1)}, u32[]{:S(2)}, u32[]{:S(2)}) %all-to-all-start.4) | async-done | bytes 16416 | tf_op jit(solution)/shard_map/all_to_all | solution.py:278
  154.8 0.8 home.1
  (2 shorter events, 0.0 us)
Async XLA Ops:
  0.0 8.3 %copy-start = (f32[4,32]{1,0:T(4,128)S(1)}, f32[4,32]{1,0:T(4,128)}, u32[]{:S(2)}) copy-start(f32[4,32]{1,0:T(4,128)} %param.11) | copy-start | bytes 1540
  1.4 13.1 %all-to-all-start = ((s32[16,12,128]{2,1,0:T(8,128)}), s32[16,12,128]{2,1,0:T(8,128)S(1)}, u32[]{:S(2)}, u32[]{:S(2)}) async-start(s32[16,12,128]{2,1,0:T(8,128)} %broadcast_in_dim.8), calls=%async_computation | async-start | bytes 262144 | tf_op jit(solution)/shard_map/all_to_all | solution.py:278
  26.0 60.4 %all-to-all-start.1 = ((bf16[16,24,6144]{2,1,0:T(8,128)(2,1)}), bf16[16,24,6144]{2,1,0:T(8,128)(2,1)}, u32[]{:S(2)}, u32[]{:S(2)}) async-start(bf16[16,24,6144]{2,1,0:T(8,128)(2,1)} %z_gather.1), calls=%async_computation.1 | async-start | bytes 9437184 | tf_op jit(solution)/shard_map/all_to_all | solution.py:278
  31.0 3.7 %copy-start.1 = (bf16[1,288,16384]{2,1,0:T(8,128)(2,1)S(1)}, bf16[1,288,16384]{2,1,0:T(8,128)(2,1)}, u32[]{:S(2)}) copy-start(bf16[1,288,16384]{2,1,0:T(8,128)(2,1)} %props_ref.3) | copy-start | bytes 28311556
  99.6 30.4 %copy-start.4 = (s32[512,1]{0,1:T(1,128)S(1)}, s32[512,1]{0,1:T(1,128)}, u32[]{:S(2)}) copy-start(s32[512,1]{0,1:T(1,128)} %param.12) | copy-start | bytes 6148
  99.6 40.1 %copy-start.2 = (bf16[320,768]{1,0:T(8,128)(2,1)S(1)}, bf16[320,768]{1,0:T(8,128)(2,1)}, u32[]{:S(2)}) copy-start(bf16[320,768]{1,0:T(8,128)(2,1)} %constant.63.clone.spread_ref) | copy-start | bytes 1474564
  99.6 40.0 %copy-start.3 = (bf16[1024,64]{1,0:T(8,128)(2,1)S(1)}, bf16[1024,64]{1,0:T(8,128)(2,1)}, u32[]{:S(2)}) copy-start(bf16[1024,64]{1,0:T(8,128)(2,1)} %constant.62.clone.fold_ref) | copy-start | bytes 393220
  122.7 16.9 %all-to-all-start.3 = ((f32[8,160,128]{2,1,0:T(8,128)}), f32[8,160,128]{2,1,0:T(8,128)S(1)}, u32[]{:S(2)}, u32[]{:S(2)}) async-start(f32[8,160,128]{2,1,0:T(8,128)} %broadcast_in_dim.11), calls=%async_computation.3 | async-start | bytes 1310720 | tf_op jit(solution)/shard_map/all_to_all | solution.py:278
  142.2 12.6 %all-to-all-start.4 = ((f32[16,2,128]{2,1,0:T(2,128)}), f32[16,2,128]{2,1,0:T(2,128)S(1)}, u32[]{:S(2)}, u32[]{:S(2)}) async-start(f32[16,2,128]{2,1,0:T(2,128)} %amplitudes.1), calls=%async_computation.4 | async-start | bytes 32768 | tf_op jit(solution)/shard_map/all_to_all | solution.py:278

commit v3 on v2

--- a/solution.py
+++ b/solution.py
@@ -15,21 +15,39 @@
     return jnp.where(rows == idx_row, 1.0, 0.0).astype(jnp.bfloat16)
 
 
-def z_gather_kernel(idx_ref, props_ref, after_ref, out_ref, held_ref, sems):
+def z_gather_kernel(idx_ref, props_ref, after_ref, out_ref, block_ref, held_ref, in_sems, out_sems):
     slabs = out_ref.shape[0]
     count = out_ref.shape[2] // NSC
-
-    def send(t):
-        return pltpu.make_async_copy(held_ref.at[t], out_ref.at[t], sems.at[t])
-
-    sites = props_ref.shape[2] // slabs
+    steps = block_ref.shape[0]
+    per = slabs // steps
+    lanes = block_ref.shape[2]
+    sites = lanes // per
     half = NSC * NSC
-
-    def pair_of_slabs(u, carry):
-        for t in (2 * u, 2 * u + 1):
+    ahead = 3
+
+    def fetch(u):
+        at = pl.ds(pl.multiple_of(u * lanes, lanes), lanes)
+        return pltpu.make_async_copy(props_ref.at[0, :, at], block_ref.at[u], in_sems.at[u])
+
+    def send(u):
+        at = pl.ds(u * per, per)
+        return pltpu.make_async_copy(held_ref.at[at], out_ref.at[at], out_sems.at[u])
+
+    for u in range(ahead):
+        fetch(u).start()
+
+    def step(u, carry):
+        fetch(u).wait()
+
+        @pl.when(u + ahead < steps)
+        def _():
+            fetch(u + ahead).start()
+
+        for k in range(per):
+            t = u * per + k
             idx = idx_ref[t]
             hot = jnp.concatenate([one_hot_columns(idx[r : r + 1, :], sites) for r in range(4)], axis=1)
-            block = props_ref[0, :, pl.ds(pl.multiple_of(t * sites, sites), sites)]
+            block = block_ref[u, :, k * sites : (k + 1) * sites]
             picked = jnp.dot(block, hot, preferred_element_type=jnp.float32)
             for l in range(NSC):
                 re, im = l * NSC, half + l * NSC
@@ -42,12 +60,12 @@
                     ],
                     axis=0,
                 ).astype(jnp.bfloat16)
-            send(t).start()
+        send(u).start()
         return carry
 
-    lax.fori_loop(0, slabs // 2, pair_of_slabs, 0)
-    for t in range(slabs):
-        send(t).wait()
+    lax.fori_loop(0, steps, step, 0)
+    for u in range(steps):
+        send(u).wait()
 
 
 def pair_pick_kernel(me_ref, idx_ref, props_ref, out_ref):
@@ -84,7 +102,42 @@
     return carry
 
 
-def combo_kernel(x_ref, w_ref, after_ref, out_ref, held_ref, acc_ref, sems):
+def coded(sums):
+    groups, rows, lanes = sums.shape
+    lane = lax.broadcasted_iota(jnp.int32, (groups, lanes), 1)
+    tail_row = lax.broadcasted_iota(jnp.int32, (groups, 16, lanes), 1)
+    tail = jnp.zeros((groups, 16, lanes), jnp.int32)
+    whole = []
+    for c in range(rows // 40):
+        part = sums[:, 40 * c : 40 * c + 40, :]
+        peak = jnp.max(jnp.abs(part), axis=1)
+        for d in (4, 2, 1):
+            other = jnp.where(
+                lane % (2 * d) < d, pltpu.roll(peak, lanes - d, 1), pltpu.roll(peak, d, 1)
+            )
+            peak = jnp.maximum(peak, other)
+        shift = 14.0 - jnp.floor(jnp.log2(jnp.maximum(peak, 2.0**-112)))
+        value = jnp.floor(part * jnp.exp2(shift)[:, None, :] + 0.5)
+        whole.append(jnp.clip(value, -32767.0, 32767.0).astype(jnp.int32))
+        tail = jnp.where(tail_row == c, shift.astype(jnp.int32)[:, None, :], tail)
+    return jnp.concatenate(whole + [tail], axis=1).astype(jnp.int16)
+
+
+def decoded_sum(coded_ref):
+    total = None
+    for g in range(coded_ref.shape[0]):
+        value = coded_ref[g].astype(jnp.int32).astype(jnp.float32)
+        rows = value.shape[0] - 16
+        parts = []
+        for c in range(rows // 40):
+            scale = jnp.exp2(-value[rows + c : rows + c + 1, :])
+            parts.append(value[40 * c : 40 * c + 40, :] * scale)
+        term = jnp.concatenate(parts, axis=0)
+        total = term if total is None else total + term
+    return total
+
+
+def combo_kernel(x_ref, w_ref, after_a, after_b, after_c, out_ref, held_ref, acc_ref, last_ref, sums_ref, sems):
     sources, _, lanes = x_ref.shape
     classes, count = w_ref.shape
     per = 4
@@ -105,24 +158,27 @@
             [wide[:, 8 * t : 8 * t + 8, :].reshape(n, depth) for t in range(3)], axis=0
         )
         right = rows.astype(jnp.bfloat16)
+        scaled = [
+            rows * jnp.concatenate([w_ref[c : c + 1, :]] * per, axis=1) for c in range(classes)
+        ]
         left = jnp.concatenate(
-            [
-                (rows * jnp.concatenate([w_ref[c : c + 1, :]] * per, axis=1)).astype(jnp.bfloat16)
-                for c in range(classes)
-            ],
-            axis=0,
-        )
-        part = lax.dot_general(
-            left, right, (((1,), (1,)), ((), ())), preferred_element_type=jnp.float32
+            [scaled[c][n * t : n * t + n, :] for t in range(3) for c in range(classes)], axis=0
+        ).astype(jnp.bfloat16)
+        contract = (((1,), (1,)), ((), ()))
+        main = lax.dot_general(left, right[0 : 2 * n], contract, preferred_element_type=jnp.float32)
+        last = lax.dot_general(
+            left[2 * classes * n :], right[2 * n :], contract, preferred_element_type=jnp.float32
         )
 
         @pl.when(s == 0)
         def _():
-            acc_ref[...] = part
+            acc_ref[...] = main
+            last_ref[...] = last
 
         @pl.when(s > 0)
         def _():
-            acc_ref[...] += part
+            acc_ref[...] += main
+            last_ref[...] += last
 
         return carry
 
@@ -139,22 +195,28 @@
 
     for c in range(classes):
 
-        def blk(a_tile, b_tile):
-            at = c * 3 * n + n * b_tile
-            return acc_ref[at : at + n, n * a_tile : n * a_tile + n]
-
-        re = blk(0, 0) + blk(1, 1)
-        im = blk(1, 0) - blk(0, 1)
-        a, b = blk(0, 2), swap_rows(blk(1, 2))
-        wide_col = jnp.where(low_row, a + b, b - a)
-        a, b = blk(2, 0), swap_lanes(blk(2, 1))
-        tall_row = jnp.where(low_lane, a + b, a - b)
-        a = blk(2, 2)
+        def blk(left_tile, right_tile):
+            at = (left_tile * classes + c) * n
+            return acc_ref[at : at + n, n * right_tile : n * right_tile + n]
+
+        re = (blk(0, 0) + blk(1, 1)).T
+        im = (blk(0, 1) - blk(1, 0)).T
+        a, b = blk(2, 0), swap_rows(blk(2, 1))
+        wide_col = jnp.where(low_row, a + b, b - a).T
+        tall_row = jnp.where(low_row, a + b, a - b)
+        a = last_ref[c * n : c * n + n, :]
         b = swap_lanes(swap_rows(a))
-        corner = jnp.where(low_row, jnp.where(low_lane, a + b, a - b), 0.0)
+        corner = jnp.where(low_row, jnp.where(low_lane, a + b, a - b), 0.0).T
         for k, m in enumerate((re, im, wide_col, tall_row, corner)):
             at = (c * 5 + k) * 8
-            out_ref[:, at : at + 8, :] = m.T.reshape(sources, 8, n)
+            sums_ref[:, at : at + 8, :] = m.reshape(sources, 8, n)
+    out_ref[...] = coded(sums_ref[...])
+
+
+def reduce_kernel(coded_ref, out_ref):
+    total = coded(decoded_sum(coded_ref)[None])
+    for g in range(out_ref.shape[0]):
+        out_ref[g] = total[0]
 
 
 def spread_matrix():
@@ -190,7 +252,7 @@
 def amplitude_kernel(sums_ref, fold_ref, spread_ref, partner_ref, out_ref):
     classes, sources = 4, 16
     combos = classes * sources
-    sums = jnp.sum(sums_ref[...], axis=0)
+    sums = decoded_sum(sums_ref)
     own = (
         lax.broadcasted_iota(jnp.int32, (sources, 128), 1) // 8
         == lax.broadcasted_iota(jnp.int32, (sources, 128), 0)
@@ -285,16 +347,19 @@
     ).astype(jnp.float32)
     weights = jnp.dot(kernel_table, one_hot, precision=lax.Precision.HIGHEST)
 
+    steps = slabs // 2
     z_rows = pl.pallas_call(
         z_gather_kernel,
-        in_specs=[IN_VMEM, IN_VMEM, pl.BlockSpec(memory_space=pl.ANY)],
+        in_specs=[IN_VMEM, pl.BlockSpec(memory_space=pl.ANY), pl.BlockSpec(memory_space=pl.ANY)],
         out_specs=pl.BlockSpec(memory_space=pl.ANY),
         out_shape=jax.ShapeDtypeStruct((slabs, 24, depth), jnp.bfloat16),
         scratch_shapes=[
+            pltpu.VMEM((steps, rows, slabs // steps * site_count), jnp.bfloat16),
             pltpu.VMEM((slabs, 24, depth), jnp.bfloat16),
-            pltpu.SemaphoreType.DMA((slabs,)),
+            pltpu.SemaphoreType.DMA((steps,)),
+            pltpu.SemaphoreType.DMA((steps,)),
         ],
-        compiler_params=params(52),
+        compiler_params=params(50),
         cost_estimate=pl.CostEstimate(
             flops=2 * rows * site_count * z_count * slabs, bytes_accessed=15_000_000, transcendentals=0
         ),
@@ -321,16 +386,19 @@
         (combo_ids[:, None] == combo_ids[None, :]) & (counter[None, :] < counter[:, None]), axis=1
     )
     slot = combo_ids // 256 * 16 + combo_ids % 16 + jnp.where(second, 64, 0)
-    source = combo_ids // 16 % 16
+    slot = slot.reshape(1, -1)
+    source = (combo_ids // 16 % 16).reshape(1, -1)
 
     sums = pl.pallas_call(
         combo_kernel,
-        in_specs=[pl.BlockSpec(memory_space=pl.ANY), IN_VMEM, pl.BlockSpec(memory_space=pl.ANY)],
+        in_specs=[pl.BlockSpec(memory_space=pl.ANY), IN_VMEM] + [pl.BlockSpec(memory_space=pl.ANY)] * 3,
         out_specs=IN_VMEM,
-        out_shape=jax.ShapeDtypeStruct((slabs, classes * 40, 128), jnp.float32),
+        out_shape=jax.ShapeDtypeStruct((slabs, classes * 40 + 16, 128), jnp.int16),
         scratch_shapes=[
             pltpu.VMEM((3, slabs, 24, depth // 3), jnp.bfloat16),
-            pltpu.VMEM((classes * slabs * 24, slabs * 24), jnp.float32),
+            pltpu.VMEM((classes * slabs * 24, slabs * 16), jnp.float32),
+            pltpu.VMEM((classes * slabs * 8, slabs * 8), jnp.float32),
+            pltpu.VMEM((slabs, classes * 40, 128), jnp.float32),
             pltpu.SemaphoreType.DMA((3,)),
         ],
         compiler_params=params(32),
@@ -338,10 +406,17 @@
             flops=2 * classes * 384 * 384 * depth, bytes_accessed=6_000_000, transcendentals=0
         ),
         name="combo_sums",
-    )(z_rows, weights, partner)
-
-    sums = jnp.sum(exchange(sums, "ta"), axis=0)
-    sums = exchange(jnp.broadcast_to(sums[None], (blocks,) + sums.shape), "sa")
+    )(z_rows, weights, partner, slot, source)
+
+    sums = pl.pallas_call(
+        reduce_kernel,
+        in_specs=[IN_VMEM],
+        out_specs=IN_VMEM,
+        out_shape=jax.ShapeDtypeStruct((blocks,) + sums.shape[1:], jnp.int16),
+        compiler_params=params(16),
+        name="reduce_sums",
+    )(exchange(sums, "ta"))
+    sums = exchange(sums, "sa")
 
     found = pl.pallas_call(
         amplitude_kernel,
@@ -364,7 +439,7 @@
         out_shape=jax.ShapeDtypeStruct((2, pair_count), jnp.float32),
         compiler_params=params(16),
         name="home",
-    )(back, slot.reshape(1, -1), source.reshape(1, -1))
+    )(back, slot, source)
 
 
 def solution(mesh):

time: 156 us -> 140 us (0.90)
  blocking collectives: 22.2 us -> 42 us
  waiting for transfers between devices: 62.9 us -> 47.3 us
  starting transfers between devices: 25.8 us -> 11.9 us
  Pallas kernels: 37.4 us -> 32 us
    all_to_all x1 -> x3, blocking collectives: 22.2 us -> 42 us  [exchange(): return lax.all_to_all(array, axis, split_axis=0, concat_axis=0, tiled=True)]
    all_to_all x4 -> x2, waiting for transfers between devices: 62.9 us -> 47.3 us  [exchange(): return lax.all_to_all(array, axis, split_axis=0, concat_axis=0, tiled=True)]
    all_to_all x4 -> x2, starting transfers between devices: 25.8 us -> 11.9 us  [exchange(): return lax.all_to_all(array, axis, split_axis=0, concat_axis=0, tiled=True)]
    pallas_call x1, Pallas kernels: 13.2 us -> 10.3 us  [local(): pl.pallas_call(combo_kernel, in_specs=[pl.BlockSpec(memory_space=pl.ANY),...]
    pallas_call x1 -> x2, Pallas kernels: 11.6 us -> 9.67 us  [the longest x1 9.21 us: local(): pl.pallas_call(z_gather_kernel, in_specs=[IN_VMEM, pl.BlockSpec(memory_sp...]
  transfers between devices with their start and end apart: 4 -> 2, of which waited for: 4 -> 2; matrix products, arithmetic and copies ran while one was open for 1% -> 1% of each run, Pallas kernels for 6% -> 7%
where the time goes in v3:
time: 140 us; the launch traced here: 139 us
  waiting for transfers between devices  47.3 us (34%)
  blocking collectives  42 us (30%)
  Pallas kernels  32 us (23%)
  starting transfers between devices  11.9 us (8%)
  local copies, waits for them, and re-layouts  4.36 us (3%)
    all_to_all x2, waiting for transfers between devices, exchange(): return lax.all_to_all(array, axis, split_axis=0, concat_axis=0, tiled=True)  47.3 us
    all_to_all x3, blocking collectives, exchange(): return lax.all_to_all(array, axis, split_axis=0, concat_axis=0, tiled=True)  42 us
    all_to_all x2, starting transfers between devices, exchange(): return lax.all_to_all(array, axis, split_axis=0, concat_axis=0, tiled=True)  11.9 us
    pallas_call x1, Pallas kernels, local(): pl.pallas_call(combo_kernel, in_specs=[pl.BlockSpec(memory_space=pl.ANY),...  10.3 us
    pallas_call x1, Pallas kernels, local(): pl.pallas_call(pair_pick_kernel, in_specs=[pl.BlockSpec(memory_space=pltp...  9.38 us
    pallas_call x1, Pallas kernels, local(): pl.pallas_call(z_gather_kernel, in_specs=[IN_VMEM, pl.BlockSpec(memory_sp...  9.21 us
    unnamed x10, local copies, waits for them, and re-layouts  3.69 us
  transfers between devices with their start and end apart: 2, of which 2 were waited for; matrix products, arithmetic and copies ran while one was open for 1% of the time, Pallas kernels for 7%

profile of v3, /device:TPU:1, one launch (start us, length us, event | category | flops | bytes accessed | tf_op | source)
XLA Modules:
  0.0 139.5 jit_solution(12466553549591016550)
XLA Ops:
  0.0 0.0 copy-start
  0.0 0.7 pad_add_fusion
  0.7 0.7 broadcast_in_dim.6
  1.4 6.9 %all-to-all-start = ((s32[16,12,128]{2,1,0:T(8,128)}), s32[16,12,128]{2,1,0:T(8,128)S(1)}, u32[]{:S(2)}, u32[]{:S(2)}) async-start(s32[16,12,128]{2,1,0:T(8,128)} %broadcast_in_dim.6), calls=%async_computation | async-start | bytes 262144 | tf_op jit(solution)/shard_map/all_to_all | solution.py:340
  8.3 0.0 copy-done
  8.3 0.8 convolution_bitcast_fusion.after_ref.w_ref
  9.1 5.3 %all-to-all-done.idx_ref = s32[16,12,128]{2,1,0:T(8,128)S(1)} async-done(((s32[16,12,128]{2,1,0:T(8,128)}), s32[16,12,128]{2,1,0:T(8,128)S(1)}, u32[]{:S(2)}, u32[]{:S(2)}) %all-to-all-start) | async-done | bytes 98336 | tf_op jit(solution)/shard_map/all_to_all | solution.py:340
  14.5 9.2 %z_gather.1 = bf16[16,24,6144]{2,1,0:T(8,128)(2,1)} custom-call(s32[16,12,128]{2,1,0:T(8,128)S(1)} %all-to-all-done.idx_ref, bf16[1,288,16384]{2,1,0:T(8,128)(2,1)} %props_ref.3, f32[4,512]{1,0:T(4,128)S(1)} %convolution_bitcast_fusion.after_ref.w_ref), custom_call_target="tpu_custom_call" | custom-call | flops 4831838208 | bytes 15000000 | tf_op jit(solution)/shard_map/z_gather/pallas_call | solution.py:351
  23.7 0.0 copy-start.4
  23.7 5.0 %all-to-all-start.1 = ((bf16[16,24,6144]{2,1,0:T(8,128)(2,1)}), bf16[16,24,6144]{2,1,0:T(8,128)(2,1)}, u32[]{:S(2)}, u32[]{:S(2)}) async-start(bf16[16,24,6144]{2,1,0:T(8,128)(2,1)} %z_gather.1), calls=%async_computation.1 | async-start | bytes 9437184 | tf_op jit(solution)/shard_map/all_to_all | solution.py:340
  28.7 0.0 copy-done.4
  28.7 0.2 fusion.1
  29.0 0.0 copy-start.1
  29.0 3.7 %copy-done.1 = bf16[1,288,16384]{2,1,0:T(8,128)(2,1)S(1)} copy-done((bf16[1,288,16384]{2,1,0:T(8,128)(2,1)S(1)}, bf16[1,288,16384]{2,1,0:T(8,128)(2,1)}, u32[]{:S(2)}) %copy-start.1) | copy-done | bytes 9437208
  32.6 9.4 %pair_pick.1.after_a.partner_ref = bf16[288,2048]{1,0:T(8,128)(2,1)S(1)} custom-call(s32[1]{0:T(128)} %bitcast.4.me_ref, s32[16,12,128]{2,1,0:T(8,128)S(1)} %all-to-all-done.idx_ref, bf16[1,288,16384]{2,1,0:T(8,128)(2,1)S(1)} %copy-done.1), custom_call_target="tpu_custom_call" | custom-call | flops 1207959552 | bytes 11000000 | tf_op jit(solution)/shard_map/pair_pick/pallas_call | solution.py:371
  42.0 42.0 %all-to-all-done.1.x_ref = bf16[16,24,6144]{2,1,0:T(8,128)(2,1)} async-done(((bf16[16,24,6144]{2,1,0:T(8,128)(2,1)}), bf16[16,24,6144]{2,1,0:T(8,128)(2,1)}, u32[]{:S(2)}, u32[]{:S(2)}) %all-to-all-start.1) | async-done | bytes 4718624 | tf_op jit(solution)/shard_map/all_to_all | solution.py:340
  84.0 0.0 copy-start.2
  84.0 0.0 copy-start.3
  84.0 10.3 %combo_sums.1 = s16[16,176,128]{2,1,0:T(8,128)(2,1)S(1)} custom-call(bf16[16,24,6144]{2,1,0:T(8,128)(2,1)} %all-to-all-done.1.x_ref, f32[4,512]{1,0:T(4,128)S(1)} %convolution_bitcast_fusion.after_ref.w_ref, bf16[288,2048]{1,0:T(8,128)(2,1)S(1)} %pair_pick.1.after_a.partner_ref, s32[1,512]{1,0:T(1,128)S(1)} %get-tuple-element.6.after_b.slot_ref, ...), custom_call_target="tpu_custom_call" | custom-call | flops 7247757312 | bytes 6000000 | tf_op jit(solution)/shard_map/combo_sums/pallas_call | solution.py:392
  94.4 15.9 %all_to_all.25.coded_ref = s16[16,176,128]{2,1,0:T(8,128)(2,1)S(1)} all-to-all(s16[16,176,128]{2,1,0:T(8,128)(2,1)S(1)} %combo_sums.1), channel_id=1, replica_groups=mesh['ta'=16,'sa'=8] {'ta'}, dimensions={0} | all-to-all | bytes 1441792 | tf_op jit(solution)/shard_map/all_to_all | solution.py:340
  110.3 0.5 reduce_sums.1
  110.8 15.3 %all_to_all.26.sums_ref = s16[8,176,128]{2,1,0:T(8,128)(2,1)S(1)} all-to-all(s16[8,176,128]{2,1,0:T(8,128)(2,1)S(1)} %reduce_sums.1), channel_id=1, replica_groups=mesh['ta'=16,'sa'=8] {'sa'}, dimensions={0} | all-to-all | bytes 720896 | tf_op jit(solution)/shard_map/all_to_all | solution.py:340
  126.0 0.0 copy-done.2
  126.0 0.0 copy-done.3
  126.0 1.9 %amplitudes.1 = f32[16,2,128]{2,1,0:T(2,128)S(1)} custom-call(s16[8,176,128]{2,1,0:T(8,128)(2,1)S(1)} %all_to_all.26.sums_ref, bf16[1024,64]{1,0:T(8,128)(2,1)S(1)} %copy-done.3, bf16[320,768]{1,0:T(8,128)(2,1)S(1)} %copy-done.2, bf16[288,2048]{1,0:T(8,128)(2,1)S(1)} %pair_pick.1.after_a.partner_ref), custom_call_target="tpu_custom_call" | custom-call | tf_op jit(solution)/shard_map/amplitudes/pallas_call | solution.py:421
  127.9 10.8 %all_to_all.27.back_ref = f32[16,2,128]{2,1,0:T(2,128)S(1)} all-to-all(f32[16,2,128]{2,1,0:T(2,128)S(1)} %amplitudes.1), channel_id=1, replica_groups=mesh['ta'=16,'sa'=8] {'ta'}, dimensions={0} | all-to-all | bytes 32768 | tf_op jit(solution)/shard_map/all_to_all | solution.py:340
  138.7 0.8 home.1
  (2 shorter events, 0.0 us)
Async XLA Ops:
  0.0 8.3 %copy-start = (f32[4,32]{1,0:T(4,128)S(1)}, f32[4,32]{1,0:T(4,128)}, u32[]{:S(2)}) copy-start(f32[4,32]{1,0:T(4,128)} %param.11) | copy-start | bytes 1540
  1.4 13.1 %all-to-all-start = ((s32[16,12,128]{2,1,0:T(8,128)}), s32[16,12,128]{2,1,0:T(8,128)S(1)}, u32[]{:S(2)}, u32[]{:S(2)}) async-start(s32[16,12,128]{2,1,0:T(8,128)} %broadcast_in_dim.6), calls=%async_computation | async-start | bytes 262144 | tf_op jit(solution)/shard_map/all_to_all | solution.py:340
  23.7 5.0 %copy-start.4 = (s32[512,1]{0,1:T(1,128)S(1)}, s32[512,1]{0,1:T(1,128)}, u32[]{:S(2)}) copy-start(s32[512,1]{0,1:T(1,128)} %param.12) | copy-start | bytes 6148
  23.7 60.4 %all-to-all-start.1 = ((bf16[16,24,6144]{2,1,0:T(8,128)(2,1)}), bf16[16,24,6144]{2,1,0:T(8,128)(2,1)}, u32[]{:S(2)}, u32[]{:S(2)}) async-start(bf16[16,24,6144]{2,1,0:T(8,128)(2,1)} %z_gather.1), calls=%async_computation.1 | async-start | bytes 9437184 | tf_op jit(solution)/shard_map/all_to_all | solution.py:340
  29.0 3.7 %copy-start.1 = (bf16[1,288,16384]{2,1,0:T(8,128)(2,1)S(1)}, bf16[1,288,16384]{2,1,0:T(8,128)(2,1)}, u32[]{:S(2)}) copy-start(bf16[1,288,16384]{2,1,0:T(8,128)(2,1)} %props_ref.3) | copy-start | bytes 28311556
  84.0 42.0 %copy-start.2 = (bf16[320,768]{1,0:T(8,128)(2,1)S(1)}, bf16[320,768]{1,0:T(8,128)(2,1)}, u32[]{:S(2)}) copy-start(bf16[320,768]{1,0:T(8,128)(2,1)} %constant.61.clone.spread_ref) | copy-start | bytes 1474564
  84.0 42.0 %copy-start.3 = (bf16[1024,64]{1,0:T(8,128)(2,1)S(1)}, bf16[1024,64]{1,0:T(8,128)(2,1)}, u32[]{:S(2)}) copy-start(bf16[1024,64]{1,0:T(8,128)(2,1)} %constant.60.clone.fold_ref) | copy-start | bytes 393220

commit v4 on v3

--- a/solution.py
+++ b/solution.py
@@ -9,20 +9,119 @@
 from jax.sharding import PartitionSpec as P
 
 NSC = 12
+MAIN = 384
+SENT = 448
 
 def one_hot_columns(idx_row, count):
     rows = lax.broadcasted_iota(jnp.int32, (count, idx_row.shape[1]), 0)
     return jnp.where(rows == idx_row, 1.0, 0.0).astype(jnp.bfloat16)
 
 
+def doubled(row, upper):
+    other = pltpu.roll(row, 64, 1)
+    low = lax.broadcasted_iota(jnp.int32, row.shape, 1) < 64
+    return jnp.where(low, other, row) if upper else jnp.where(low, row, other)
+
+
+def as_column(row):
+    eye = lax.broadcasted_iota(jnp.int32, (128, 128), 0) == lax.broadcasted_iota(jnp.int32, (128, 128), 1)
+    return jnp.sum(jnp.where(eye, row, 0.0), axis=1, keepdims=True)
+
+
+def list_kernel(z_hbm, site_hbm, combo_hbm, out_ref, z_ref, site_ref, combo_ref, sems):
+    copies = [
+        pltpu.make_async_copy(source, held, sems.at[k])
+        for k, (source, held) in enumerate(((z_hbm, z_ref), (site_hbm, site_ref), (combo_hbm, combo_ref)))
+    ]
+    for copy in copies:
+        copy.start()
+    for copy in copies:
+        copy.wait()
+    groups = z_ref.shape[0]
+    row = [z_ref[g : g + 1, :].astype(jnp.float32) for g in range(groups)]
+    col = [as_column(r) for r in row]
+    sub = lax.broadcasted_iota(jnp.int32, (128, 128), 0)
+    lane = lax.broadcasted_iota(jnp.int32, (128, 128), 1)
+    first_col, first_row = [], []
+    for g in range(groups):
+        again_col = jnp.where((col[g] == row[g]) & (lane < sub), 1.0, 0.0)
+        again_row = jnp.where((col[g] == row[g]) & (sub < lane), 1.0, 0.0)
+        for h in range(g):
+            again_col = jnp.maximum(again_col, jnp.where(col[g] == row[h], 1.0, 0.0))
+            again_row = jnp.maximum(again_row, jnp.where(col[h] == row[g], 1.0, 0.0))
+        first_col.append(1.0 - jnp.max(again_col, axis=1, keepdims=True))
+        first_row.append(1.0 - jnp.max(again_row, axis=0, keepdims=True))
+    count = jnp.zeros((1, 1), jnp.float32)
+    place = []
+    for g in range(groups):
+        here = jnp.sum(jnp.where(lane < sub, first_row[g], 0.0), axis=1, keepdims=True) + count
+        place.append(jnp.where(first_col[g] > 0.5, here, -1.0))
+        count = count + jnp.sum(first_row[g], axis=1, keepdims=True)
+    block = []
+    for g in range(groups):
+        want = (lane + 128 * g).astype(jnp.float32)
+        total = jnp.zeros((128, 128), jnp.float32)
+        for h in range(groups):
+            total += jnp.where(place[h] == want, col[h], 0.0)
+        found = jnp.sum(total, axis=0, keepdims=True)
+        block.append(jnp.where(want[0:1, :] < count, found, -1.0).astype(jnp.int32))
+    block += [site_ref[...], combo_ref[...]]
+    block.append(jnp.broadcast_to(count, (16 - 3 * groups, 128)).astype(jnp.int32))
+    block = jnp.concatenate(block, axis=0)
+    for t in range(out_ref.shape[0]):
+        out_ref[t] = block
+
+
+def weight_kernel(w_ref, z_ref, idx_ref, out_ref):
+    classes = w_ref.shape[0]
+    groups = z_ref.shape[0]
+    hot = []
+    for g in range(groups):
+        col = as_column(z_ref[g : g + 1, :].astype(jnp.float32))
+        hot.append(
+            jnp.concatenate(
+                [
+                    jnp.where(col == idx_ref[0, h : h + 1, :].astype(jnp.float32), 1.0, 0.0)
+                    for h in range(groups)
+                ],
+                axis=1,
+            )
+        )
+    hot = jnp.concatenate(hot, axis=0).astype(jnp.bfloat16)
+    rest = w_ref[...]
+    added = jnp.zeros(rest.shape, jnp.float32)
+    for _ in range(3):
+        part = rest.astype(jnp.bfloat16)
+        rest = rest - part.astype(jnp.float32)
+        added += jnp.dot(part, hot, preferred_element_type=jnp.float32)
+    edge = added[:, MAIN : MAIN + 128]
+    for l in range(NSC):
+        out_ref[:, l * MAIN : (l + 1) * MAIN] = added[:, 0:MAIN]
+    for k, upper in ((0, False), (1, True)):
+        for m in range(NSC // 2):
+            at = NSC * (MAIN + 64 * k) + 128 * m
+            out_ref[:, at : at + 128] = doubled(edge, upper)
+
+
+def ordered_rows(picked, l):
+    re, im = l * NSC, NSC * NSC + l * NSC
+    return jnp.concatenate(
+        [picked[re : re + 8], picked[im : im + 8], picked[re + 8 : re + 12], picked[im + 8 : im + 12]],
+        axis=0,
+    )
+
+
+def two_to_a_tile(picked, l):
+    low = lax.broadcasted_iota(jnp.int32, (24, 128), 1) < 64
+    return jnp.where(low, ordered_rows(picked, l), ordered_rows(picked, l + 1)).astype(jnp.bfloat16)
+
+
 def z_gather_kernel(idx_ref, props_ref, after_ref, out_ref, block_ref, held_ref, in_sems, out_sems):
     slabs = out_ref.shape[0]
-    count = out_ref.shape[2] // NSC
     steps = block_ref.shape[0]
     per = slabs // steps
     lanes = block_ref.shape[2]
     sites = lanes // per
-    half = NSC * NSC
     ahead = 3
 
     def fetch(u):
@@ -46,26 +145,30 @@
         for k in range(per):
             t = u * per + k
             idx = idx_ref[t]
-            hot = jnp.concatenate([one_hot_columns(idx[r : r + 1, :], sites) for r in range(4)], axis=1)
+            rows = [idx[r : r + 1, :] for r in range(3)] + [doubled(idx[3:4, :], False)]
+            hot = jnp.concatenate([one_hot_columns(r, sites) for r in rows], axis=1)
             block = block_ref[u, :, k * sites : (k + 1) * sites]
             picked = jnp.dot(block, hot, preferred_element_type=jnp.float32)
             for l in range(NSC):
-                re, im = l * NSC, half + l * NSC
-                held_ref[t, :, l * count : (l + 1) * count] = jnp.concatenate(
-                    [
-                        picked[re : re + 8],
-                        picked[im : im + 8],
-                        picked[re + 8 : re + 12],
-                        picked[im + 8 : im + 12],
-                    ],
-                    axis=0,
-                ).astype(jnp.bfloat16)
+                held_ref[t, :, l * MAIN : (l + 1) * MAIN] = ordered_rows(picked[:, 0:MAIN], l).astype(
+                    jnp.bfloat16
+                )
+            for l in range(0, NSC, 2):
+                at = NSC * MAIN + 64 * l
+                held_ref[t, :, at : at + 128] = two_to_a_tile(picked[:, MAIN : MAIN + 128], l)
         send(u).start()
         return carry
 
     lax.fori_loop(0, steps, step, 0)
     for u in range(steps):
         send(u).wait()
+
+
+def rest_gather_kernel(idx_ref, props_ref, out_ref):
+    hot = one_hot_columns(doubled(idx_ref[0, 3:4, :], True), props_ref.shape[2])
+    picked = jnp.dot(props_ref[0], hot, preferred_element_type=jnp.float32)
+    for l in range(0, NSC, 2):
+        out_ref[0, :, 64 * l : 64 * l + 128] = two_to_a_tile(picked, l)
 
 
 def pair_pick_kernel(me_ref, idx_ref, props_ref, out_ref):
@@ -137,11 +240,14 @@
     return total
 
 
-def combo_kernel(x_ref, w_ref, after_a, after_b, after_c, out_ref, held_ref, acc_ref, last_ref, sums_ref, sems):
+def combo_kernel(
+    more_ref, x_ref, rest_ref, w_ref, after_a, after_b, after_c,
+    out_ref, held_ref, rest_held, acc_ref, last_ref, sums_ref, sems,
+):
     sources, _, lanes = x_ref.shape
-    classes, count = w_ref.shape
-    per = 4
-    depth = per * count
+    classes = w_ref.shape[0]
+    depth = held_ref.shape[3]
+    rest_depth = rest_held.shape[2]
     n = sources * 8
 
     def piece(s):
@@ -151,16 +257,12 @@
     for s in range(lanes // depth):
         piece(s).start()
 
-    def chunk(s, carry):
-        piece(s).wait()
-        wide = held_ref[s].astype(jnp.float32)
+    def products(wide, weights):
         rows = jnp.concatenate(
-            [wide[:, 8 * t : 8 * t + 8, :].reshape(n, depth) for t in range(3)], axis=0
+            [wide[:, 8 * t : 8 * t + 8, :].reshape(n, wide.shape[2]) for t in range(3)], axis=0
         )
         right = rows.astype(jnp.bfloat16)
-        scaled = [
-            rows * jnp.concatenate([w_ref[c : c + 1, :]] * per, axis=1) for c in range(classes)
-        ]
+        scaled = [rows * weights[c : c + 1, :] for c in range(classes)]
         left = jnp.concatenate(
             [scaled[c][n * t : n * t + n, :] for t in range(3) for c in range(classes)], axis=0
         ).astype(jnp.bfloat16)
@@ -169,6 +271,12 @@
         last = lax.dot_general(
             left[2 * classes * n :], right[2 * n :], contract, preferred_element_type=jnp.float32
         )
+        return main, last
+
+    def chunk(s, carry):
+        piece(s).wait()
+        at = pl.ds(pl.multiple_of(s * depth, depth), depth)
+        main, last = products(held_ref[s].astype(jnp.float32), w_ref[:, at])
 
         @pl.when(s == 0)
         def _():
@@ -183,6 +291,15 @@
         return carry
 
     lax.fori_loop(0, lanes // depth, chunk, 0)
+
+    @pl.when(more_ref[0] > 0)
+    def _():
+        copy = pltpu.make_async_copy(rest_ref, rest_held, sems.at[lanes // depth])
+        copy.start()
+        copy.wait()
+        main, last = products(rest_held[...].astype(jnp.float32), w_ref[:, lanes : lanes + rest_depth])
+        acc_ref[...] += main
+        last_ref[...] += last
 
     low_row = lax.broadcasted_iota(jnp.int32, (n, n), 0) % 8 < 4
     low_lane = lax.broadcasted_iota(jnp.int32, (n, n), 1) % 8 < 4
@@ -334,13 +451,25 @@
     z_count = z_sites.shape[0]
     pair_count = pair_site.shape[0]
     classes = kernel_table.shape[0]
-    depth = NSC * z_count
+    depth = NSC * SENT
+    rest_depth = NSC * (z_count - SENT)
 
     def exchange(array, axis):
         return lax.all_to_all(array, axis, split_axis=0, concat_axis=0, tiled=True)
 
-    lists = jnp.concatenate([z_sites, pair_site, pair_combo[:, 0]]).reshape(1, -1, 128)
-    lists = exchange(jnp.broadcast_to(lists, (slabs,) + lists.shape[1:]), "ta")
+    z_table = z_sites.reshape(-1, 128)
+    lists = pl.pallas_call(
+        list_kernel,
+        in_specs=[pl.BlockSpec(memory_space=pl.ANY)] * 3,
+        out_specs=IN_VMEM,
+        out_shape=jax.ShapeDtypeStruct((slabs, 16, 128), jnp.int32),
+        scratch_shapes=[pltpu.VMEM((z_count // 128, 128), jnp.int32)] * 3 + [pltpu.SemaphoreType.DMA((3,))],
+        compiler_params=params(60),
+        name="lists",
+    )(z_table, pair_site.reshape(-1, 128), pair_combo.reshape(-1, 128))
+    own_list = lists[0:1]
+    lists = exchange(lists, "ta")
+    more = jnp.any(lists[:, 12, 0] > SENT)
 
     one_hot = (
         z_class[None, :] == jnp.arange(kernel_table.shape[1], dtype=jnp.int32)[:, None]
@@ -367,6 +496,36 @@
     )(lists, propagators, weights)
     z_rows = exchange(z_rows, "ta")
 
+    def send_rest(lists, propagators, blank):
+        rest = pl.pallas_call(
+            rest_gather_kernel,
+            grid=(slabs,),
+            in_specs=[
+                pl.BlockSpec((1,) + lists.shape[1:], lambda t: (t, 0, 0)),
+                pl.BlockSpec((1, rows, site_count), lambda t: (0, 0, t)),
+            ],
+            out_specs=pl.BlockSpec((1, 24, rest_depth), lambda t: (t, 0, 0)),
+            out_shape=jax.ShapeDtypeStruct((slabs, 24, rest_depth), jnp.bfloat16),
+            compiler_params=params(24),
+            name="rest_gather",
+        )(lists, propagators)
+        return exchange(rest, "ta")
+
+    def no_rest(lists, propagators, blank):
+        return blank
+
+    blank = jnp.zeros((slabs, 24, rest_depth), jnp.bfloat16)
+    after, blank, z_rows = lax.optimization_barrier((more, blank, z_rows))
+    rest_rows = lax.cond(after, send_rest, no_rest, lists, propagators, blank)
+    added = pl.pallas_call(
+        weight_kernel,
+        in_specs=[IN_VMEM] * 3,
+        out_specs=IN_VMEM,
+        out_shape=jax.ShapeDtypeStruct((classes, depth + rest_depth), jnp.float32),
+        compiler_params=params(16),
+        name="weights",
+    )(weights, z_table, own_list)
+
     slots = 128
     partner = pl.pallas_call(
         pair_pick_kernel,
@@ -391,22 +550,29 @@
 
     sums = pl.pallas_call(
         combo_kernel,
-        in_specs=[pl.BlockSpec(memory_space=pl.ANY), IN_VMEM] + [pl.BlockSpec(memory_space=pl.ANY)] * 3,
+        in_specs=[
+            pl.BlockSpec(memory_space=pltpu.SMEM),
+            pl.BlockSpec(memory_space=pl.ANY),
+            pl.BlockSpec(memory_space=pl.ANY),
+            IN_VMEM,
+        ]
+        + [pl.BlockSpec(memory_space=pl.ANY)] * 3,
         out_specs=IN_VMEM,
         out_shape=jax.ShapeDtypeStruct((slabs, classes * 40 + 16, 128), jnp.int16),
         scratch_shapes=[
             pltpu.VMEM((3, slabs, 24, depth // 3), jnp.bfloat16),
+            pltpu.VMEM((slabs, 24, rest_depth), jnp.bfloat16),
             pltpu.VMEM((classes * slabs * 24, slabs * 16), jnp.float32),
             pltpu.VMEM((classes * slabs * 8, slabs * 8), jnp.float32),
             pltpu.VMEM((slabs, classes * 40, 128), jnp.float32),
-            pltpu.SemaphoreType.DMA((3,)),
+            pltpu.SemaphoreType.DMA((4,)),
         ],
         compiler_params=params(32),
         cost_estimate=pl.CostEstimate(
             flops=2 * classes * 384 * 384 * depth, bytes_accessed=6_000_000, transcendentals=0
         ),
         name="combo_sums",
-    )(z_rows, weights, partner, slot, source)
+    )(more.astype(jnp.int32).reshape(1), z_rows, rest_rows, added, partner, slot, source)
 
     sums = pl.pallas_call(
         reduce_kernel,

time: 140 us -> 134 us (0.957)
  waiting for transfers between devices: 47.3 us -> 38.5 us
  Pallas kernels: 32 us -> 37.4 us
  local copies, waits for them, and re-layouts: 4.36 us -> 0.77 us
    all_to_all x2, waiting for transfers between devices: 47.3 us -> 38.5 us  [exchange(): return lax.all_to_all(array, axis, split_axis=0, concat_axis=0, tiled=True)]
    pallas_call x1, Pallas kernels: 9.38 us -> 13.1 us  [local(): pl.pallas_call(pair_pick_kernel, in_specs=[pl.BlockSpec(memory_space=pltp...]
    unnamed x10, local copies, waits for them, and re-layouts: 3.69 us -> 0.03 us
    pallas_call x1 -> x3, Pallas kernels: 10.3 us -> 11.7 us  [the longest x1 9.43 us: local(): pl.pallas_call(combo_kernel, in_specs=[pl.BlockSpec(memory_space=pltpu.SM...]
  transfers between devices with their start and end apart: 2 -> 2, of which waited for: 2 -> 2; matrix products, arithmetic and copies ran while one was open for 1% -> 2% of each run, Pallas kernels for 7% -> 10%
where the time goes in v4:
time: 134 us
  blocking collectives  42 us (31%)
  waiting for transfers between devices  38.5 us (29%)
  Pallas kernels  37.4 us (28%)
  starting transfers between devices  11.9 us (9%)
  between operations  1.42 us (1%)
    all_to_all x3, blocking collectives, exchange(): return lax.all_to_all(array, axis, split_axis=0, concat_axis=0, tiled=True)  42 us
    all_to_all x2, waiting for transfers between devices, exchange(): return lax.all_to_all(array, axis, split_axis=0, concat_axis=0, tiled=True)  38.5 us
    pallas_call x1, Pallas kernels, local(): pl.pallas_call(pair_pick_kernel, in_specs=[pl.BlockSpec(memory_space=pltp...  13.1 us
    all_to_all x2, starting transfers between devices, exchange(): return lax.all_to_all(array, axis, split_axis=0, concat_axis=0, tiled=True)  11.9 us
    pallas_call x1, Pallas kernels, local(): pl.pallas_call(z_gather_kernel, in_specs=[IN_VMEM, pl.BlockSpec(memory_sp...  9.5 us
    pallas_call x1, Pallas kernels, local(): pl.pallas_call(combo_kernel, in_specs=[pl.BlockSpec(memory_space=pltpu.SM...  9.43 us
  transfers between devices with their start and end apart: 2, of which 2 were waited for; matrix products, arithmetic and copies ran while one was open for 2% of the time, Pallas kernels for 10%

profile of v4, /device:TPU:1, one launch (start us, length us, event | category | flops | bytes accessed | tf_op | source)
XLA Modules:
  0.0 133.8 jit_solution(6389369403650717319)
XLA Ops:
  0.0 0.0 copy-start
  0.0 1.8 %lists.1 = s32[16,16,128]{2,1,0:T(8,128)} custom-call(s32[4,128]{1,0:T(4,128)} %bitcast.28, s32[4,128]{1,0:T(4,128)} %bitcast.33, s32[4,128]{1,0:T(4,128)} %bitcast.30), custom_call_target="tpu_custom_call" | custom-call | tf_op jit(solution)/shard_map/lists/pallas_call | solution.py:461
  1.9 6.9 %all-to-all-start.1 = ((s32[16,16,128]{2,1,0:T(8,128)}), s32[16,16,128]{2,1,0:T(8,128)S(1)}, u32[]{:S(2)}, u32[]{:S(2)}) async-start(s32[16,16,128]{2,1,0:T(8,128)} %lists.1), calls=%async_computation.1 | async-start | bytes 262144 | tf_op jit(solution)/shard_map/all_to_all | solution.py:458
  8.8 0.0 copy-done
  8.8 0.8 convolution_bitcast_fusion.after_ref.w_ref
  9.6 5.3 %all-to-all-done.1.idx_ref = s32[16,16,128]{2,1,0:T(8,128)S(1)} async-done(((s32[16,16,128]{2,1,0:T(8,128)}), s32[16,16,128]{2,1,0:T(8,128)S(1)}, u32[]{:S(2)}, u32[]{:S(2)}) %all-to-all-start.1) | async-done | bytes 131104 | tf_op jit(solution)/shard_map/all_to_all | solution.py:458
  14.9 9.5 %z_gather.1 = bf16[16,24,5376]{2,1,0:T(8,128)(2,1)} custom-call(s32[16,16,128]{2,1,0:T(8,128)S(1)} %all-to-all-done.1.idx_ref, bf16[1,288,16384]{2,1,0:T(8,128)(2,1)} %props_ref.3, f32[4,512]{1,0:T(4,128)S(1)} %convolution_bitcast_fusion.after_ref.w_ref), custom_call_target="tpu_custom_call" | custom-call | flops 4831838208 | bytes 15000000 | tf_op jit(solution)/shard_map/z_gather/pallas_call | solution.py:480
  24.4 0.0 copy-start.3
  24.4 0.0 copy-start.4
  24.5 4.9 %all-to-all-start.2 = ((bf16[16,24,5376]{2,1,0:T(8,128)(2,1)}), bf16[16,24,5376]{2,1,0:T(8,128)(2,1)}, u32[]{:S(2)}, u32[]{:S(2)}) async-start(bf16[16,24,5376]{2,1,0:T(8,128)(2,1)} %z_gather.1), calls=%async_computation.2 | async-start | bytes 8257536 | tf_op jit(solution)/shard_map/all_to_all | solution.py:458
  29.4 0.7 slice.9.idx_ref
  30.1 0.0 copy-done.3
  30.1 0.5 weights.1.w_ref
  30.5 0.0 copy-done.4
  30.6 0.3 fusion.1
  30.9 0.7 compare_reduce_fusion
  32.2 13.1 %pair_pick.1.after_a.partner_ref = bf16[288,2048]{1,0:T(8,128)(2,1)S(1)} custom-call(s32[1]{0:T(128)} %bitcast.5.me_ref, s32[16,16,128]{2,1,0:T(8,128)S(1)} %all-to-all-done.1.idx_ref, bf16[1,288,16384]{2,1,0:T(8,128)(2,1)} %props_ref.3), custom_call_target="tpu_custom_call" | custom-call | flops 1207959552 | bytes 11000000 | tf_op jit(solution)/shard_map/pair_pick/pallas_call | solution.py:530
  45.2 33.2 %all-to-all-done.2.x_ref = bf16[16,24,5376]{2,1,0:T(8,128)(2,1)} async-done(((bf16[16,24,5376]{2,1,0:T(8,128)(2,1)}), bf16[16,24,5376]{2,1,0:T(8,128)(2,1)}, u32[]{:S(2)}, u32[]{:S(2)}) %all-to-all-start.2) | async-done | bytes 4128800 | tf_op jit(solution)/shard_map/all_to_all | solution.py:458
  79.2 0.0 copy-start.1
  79.2 0.0 copy-start.2
  79.2 9.4 %combo_sums.1 = s16[16,176,128]{2,1,0:T(8,128)(2,1)S(1)} custom-call(s32[1]{0:T(128)} %bitcast.3.more_ref, bf16[16,24,5376]{2,1,0:T(8,128)(2,1)} %all-to-all-done.2.x_ref, bf16[16,24,768]{2,1,0:T(8,128)(2,1)S(1)} %get-tuple-element.23.rest_ref, f32[4,6144]{1,0:T(4,128)S(1)} %weights.1.w_ref, bf16[288,2048]{1,0:T(8,128)(2,1)S(1)} %pair_pick.1.after_a.partner_ref, ...), custom_call_target="tpu_custom_call" | custom-call | flops 6341787648 | bytes 6000000 | tf_op jit(solution)/shard_map/combo_sums/pallas_call | solution.py:551
  88.6 15.9 %all_to_all.30.coded_ref = s16[16,176,128]{2,1,0:T(8,128)(2,1)S(1)} all-to-all(s16[16,176,128]{2,1,0:T(8,128)(2,1)S(1)} %combo_sums.1), channel_id=1, replica_groups=mesh['ta'=16,'sa'=8] {'ta'}, dimensions={0} | all-to-all | bytes 1441792 | tf_op jit(solution)/shard_map/all_to_all | solution.py:458
  104.6 0.5 reduce_sums.1
  105.0 15.3 %all_to_all.31.sums_ref = s16[8,176,128]{2,1,0:T(8,128)(2,1)S(1)} all-to-all(s16[8,176,128]{2,1,0:T(8,128)(2,1)S(1)} %reduce_sums.1), channel_id=1, replica_groups=mesh['ta'=16,'sa'=8] {'sa'}, dimensions={0} | all-to-all | bytes 720896 | tf_op jit(solution)/shard_map/all_to_all | solution.py:458
  120.3 0.0 copy-done.1
  120.3 0.0 copy-done.2
  120.3 1.9 %amplitudes.1 = f32[16,2,128]{2,1,0:T(2,128)S(1)} custom-call(s16[8,176,128]{2,1,0:T(8,128)(2,1)S(1)} %all_to_all.31.sums_ref, bf16[1024,64]{1,0:T(8,128)(2,1)S(1)} %copy-done.2, bf16[320,768]{1,0:T(8,128)(2,1)S(1)} %copy-done.1, bf16[288,2048]{1,0:T(8,128)(2,1)S(1)} %pair_pick.1.after_a.partner_ref), custom_call_target="tpu_custom_call" | custom-call | tf_op jit(solution)/shard_map/amplitudes/pallas_call | solution.py:587
  122.2 10.8 %all_to_all.32.back_ref = f32[16,2,128]{2,1,0:T(2,128)S(1)} all-to-all(f32[16,2,128]{2,1,0:T(2,128)S(1)} %amplitudes.1), channel_id=1, replica_groups=mesh['ta'=16,'sa'=8] {'ta'}, dimensions={0} | all-to-all | bytes 32768 | tf_op jit(solution)/shard_map/all_to_all | solution.py:458
  133.0 0.8 home.1
  (4 shorter events, 0.1 us)
Async XLA Ops:
  0.0 8.8 %copy-start = (f32[4,32]{1,0:T(4,128)S(1)}, f32[4,32]{1,0:T(4,128)}, u32[]{:S(2)}) copy-start(f32[4,32]{1,0:T(4,128)} %param.13) | copy-start | bytes 1540
  1.9 13.1 %all-to-all-start.1 = ((s32[16,16,128]{2,1,0:T(8,128)}), s32[16,16,128]{2,1,0:T(8,128)S(1)}, u32[]{:S(2)}, u32[]{:S(2)}) async-start(s32[16,16,128]{2,1,0:T(8,128)} %lists.1), calls=%async_computation.1 | async-start | bytes 262144 | tf_op jit(solution)/shard_map/all_to_all | solution.py:458
  24.4 5.7 %copy-start.3 = (s32[512]{0:T(512)S(1)}, s32[512]{0:T(512)}, u32[]{:S(2)}) copy-start(s32[512]{0:T(512)} %param.11) | copy-start | bytes 6148
  24.4 6.1 %copy-start.4 = (s32[512,1]{0,1:T(1,128)S(1)}, s32[512,1]{0,1:T(1,128)}, u32[]{:S(2)}) copy-start(s32[512,1]{0,1:T(1,128)} %param.14) | copy-start | bytes 6148
  24.5 54.0 %all-to-all-start.2 = ((bf16[16,24,5376]{2,1,0:T(8,128)(2,1)}), bf16[16,24,5376]{2,1,0:T(8,128)(2,1)}, u32[]{:S(2)}, u32[]{:S(2)}) async-start(bf16[16,24,5376]{2,1,0:T(8,128)(2,1)} %z_gather.1), calls=%async_computation.2 | async-start | bytes 8257536 | tf_op jit(solution)/shard_map/all_to_all | solution.py:458
  79.2 41.1 %copy-start.1 = (bf16[320,768]{1,0:T(8,128)(2,1)S(1)}, bf16[320,768]{1,0:T(8,128)(2,1)}, u32[]{:S(2)}) copy-start(bf16[320,768]{1,0:T(8,128)(2,1)} %constant.65.clone.spread_ref) | copy-start | bytes 1474564
  79.2 41.1 %copy-start.2 = (bf16[1024,64]{1,0:T(8,128)(2,1)S(1)}, bf16[1024,64]{1,0:T(8,128)(2,1)}, u32[]{:S(2)}) copy-start(bf16[1024,64]{1,0:T(8,128)(2,1)} %constant.64.clone.fold_ref) | copy-start | bytes 393220

commit v5 on v4

--- a/solution.py
+++ b/solution.py
@@ -116,13 +116,22 @@
     return jnp.where(low, ordered_rows(picked, l), ordered_rows(picked, l + 1)).astype(jnp.bfloat16)
 
 
+def pick_sites(block, rows):
+    count, half = block.shape[0], block.shape[1] // 2
+    hot = jnp.concatenate([one_hot_columns(r % half, half) for r in rows], axis=1)
+    upper = jnp.concatenate(rows, axis=1) >= half
+    both = jnp.concatenate([block[:, 0:half], block[:, half:]], axis=0)
+    picked = jnp.dot(both, hot, preferred_element_type=jnp.float32)
+    return jnp.where(upper, picked[count:], picked[0:count])
+
+
 def z_gather_kernel(idx_ref, props_ref, after_ref, out_ref, block_ref, held_ref, in_sems, out_sems):
     slabs = out_ref.shape[0]
     steps = block_ref.shape[0]
     per = slabs // steps
     lanes = block_ref.shape[2]
     sites = lanes // per
-    ahead = 3
+    ahead = min(3, steps)
 
     def fetch(u):
         at = pl.ds(pl.multiple_of(u * lanes, lanes), lanes)
@@ -146,9 +155,7 @@
             t = u * per + k
             idx = idx_ref[t]
             rows = [idx[r : r + 1, :] for r in range(3)] + [doubled(idx[3:4, :], False)]
-            hot = jnp.concatenate([one_hot_columns(r, sites) for r in rows], axis=1)
-            block = block_ref[u, :, k * sites : (k + 1) * sites]
-            picked = jnp.dot(block, hot, preferred_element_type=jnp.float32)
+            picked = pick_sites(block_ref[u, :, k * sites : (k + 1) * sites], rows)
             for l in range(NSC):
                 held_ref[t, :, l * MAIN : (l + 1) * MAIN] = ordered_rows(picked[:, 0:MAIN], l).astype(
                     jnp.bfloat16
@@ -210,7 +217,7 @@
     lane = lax.broadcasted_iota(jnp.int32, (groups, lanes), 1)
     tail_row = lax.broadcasted_iota(jnp.int32, (groups, 16, lanes), 1)
     tail = jnp.zeros((groups, 16, lanes), jnp.int32)
-    whole = []
+    whole, corners = [], []
     for c in range(rows // 40):
         part = sums[:, 40 * c : 40 * c + 40, :]
         peak = jnp.max(jnp.abs(part), axis=1)
@@ -221,20 +228,32 @@
             peak = jnp.maximum(peak, other)
         shift = 14.0 - jnp.floor(jnp.log2(jnp.maximum(peak, 2.0**-112)))
         value = jnp.floor(part * jnp.exp2(shift)[:, None, :] + 0.5)
-        whole.append(jnp.clip(value, -32767.0, 32767.0).astype(jnp.int32))
+        value = jnp.clip(value, -32767.0, 32767.0)
+        whole.append(value[:, 0:32, :].astype(jnp.int32))
+        corner = value[:, 32:40, :]
+        if c % 2:
+            corners.append((even + pltpu.roll(corner, 4, 2)).astype(jnp.int32))
+        even = corner
         tail = jnp.where(tail_row == c, shift.astype(jnp.int32)[:, None, :], tail)
-    return jnp.concatenate(whole + [tail], axis=1).astype(jnp.int16)
+    return jnp.concatenate(whole + corners + [tail], axis=1).astype(jnp.int16)
 
 
 def decoded_sum(coded_ref):
     total = None
     for g in range(coded_ref.shape[0]):
         value = coded_ref[g].astype(jnp.int32).astype(jnp.float32)
-        rows = value.shape[0] - 16
+        rows, lanes = value.shape
+        low = lax.broadcasted_iota(jnp.int32, (8, lanes), 1) % 8 < 4
+        classes = (rows - 16) // 36
         parts = []
-        for c in range(rows // 40):
-            scale = jnp.exp2(-value[rows + c : rows + c + 1, :])
-            parts.append(value[40 * c : 40 * c + 40, :] * scale)
+        for c in range(classes):
+            scale = jnp.exp2(-value[rows - 16 + c : rows - 15 + c, :])
+            at = 32 * classes + 8 * (c // 2)
+            corner = value[at : at + 8, :]
+            if c % 2:
+                corner = pltpu.roll(corner, lanes - 4, 1)
+            parts.append(value[32 * c : 32 * c + 32, :] * scale)
+            parts.append(jnp.where(low, corner * scale, 0.0))
         term = jnp.concatenate(parts, axis=0)
         total = term if total is None else total + term
     return total
@@ -476,7 +495,7 @@
     ).astype(jnp.float32)
     weights = jnp.dot(kernel_table, one_hot, precision=lax.Precision.HIGHEST)
 
-    steps = slabs // 2
+    steps = slabs // 4
     z_rows = pl.pallas_call(
         z_gather_kernel,
         in_specs=[IN_VMEM, pl.BlockSpec(memory_space=pl.ANY), pl.BlockSpec(memory_space=pl.ANY)],
@@ -558,7 +577,7 @@
         ]
         + [pl.BlockSpec(memory_space=pl.ANY)] * 3,
         out_specs=IN_VMEM,
-        out_shape=jax.ShapeDtypeStruct((slabs, classes * 40 + 16, 128), jnp.int16),
+        out_shape=jax.ShapeDtypeStruct((slabs, classes * 36 + 16, 128), jnp.int16),
         scratch_shapes=[
             pltpu.VMEM((3, slabs, 24, depth // 3), jnp.bfloat16),
             pltpu.VMEM((slabs, 24, rest_depth), jnp.bfloat16),

time: 134 us -> 133 us (level)
  no operation moved by 1% of the time
where the time goes in v5:
time: 133 us; the launch traced here: 132 us
  blocking collectives  41.2 us (31%)
  waiting for transfers between devices  38.5 us (29%)
  Pallas kernels  36.7 us (28%)
  starting transfers between devices  11.9 us (9%)
  between operations  1.41 us (1%)
    all_to_all x3, blocking collectives, exchange(): return lax.all_to_all(array, axis, split_axis=0, concat_axis=0, tiled=True)  41.2 us
    all_to_all x2, waiting for transfers between devices, exchange(): return lax.all_to_all(array, axis, split_axis=0, concat_axis=0, tiled=True)  38.5 us
    pallas_call x1, Pallas kernels, local(): pl.pallas_call(pair_pick_kernel, in_specs=[pl.BlockSpec(memory_space=pltp...  13.1 us
    all_to_all x2, starting transfers between devices, exchange(): return lax.all_to_all(array, axis, split_axis=0, concat_axis=0, tiled=True)  11.9 us
    pallas_call x1, Pallas kernels, local(): pl.pallas_call(combo_kernel, in_specs=[pl.BlockSpec(memory_space=pltpu.SM...  9.42 us
    pallas_call x1, Pallas kernels, local(): pl.pallas_call(z_gather_kernel, in_specs=[IN_VMEM, pl.BlockSpec(memory_sp...  8.76 us
  transfers between devices with their start and end apart: 2, of which 2 were waited for; matrix products, arithmetic and copies ran while one was open for 2% of the time, Pallas kernels for 10%

profile of v5, /device:TPU:1, one launch (start us, length us, event | category | flops | bytes accessed | tf_op | source)
XLA Modules:
  0.0 132.3 jit_solution(7798345242670574502)
XLA Ops:
  0.0 0.0 copy-start
  0.0 1.8 %lists.1 = s32[16,16,128]{2,1,0:T(8,128)} custom-call(s32[4,128]{1,0:T(4,128)} %bitcast.28, s32[4,128]{1,0:T(4,128)} %bitcast.33, s32[4,128]{1,0:T(4,128)} %bitcast.30), custom_call_target="tpu_custom_call" | custom-call | tf_op jit(solution)/shard_map/lists/pallas_call | solution.py:480
  1.9 6.9 %all-to-all-start.1 = ((s32[16,16,128]{2,1,0:T(8,128)}), s32[16,16,128]{2,1,0:T(8,128)S(1)}, u32[]{:S(2)}, u32[]{:S(2)}) async-start(s32[16,16,128]{2,1,0:T(8,128)} %lists.1), calls=%async_computation.1 | async-start | bytes 262144 | tf_op jit(solution)/shard_map/all_to_all | solution.py:477
  8.8 0.0 copy-done
  8.8 0.8 convolution_bitcast_fusion.after_ref.w_ref
  9.6 5.3 %all-to-all-done.1.idx_ref = s32[16,16,128]{2,1,0:T(8,128)S(1)} async-done(((s32[16,16,128]{2,1,0:T(8,128)}), s32[16,16,128]{2,1,0:T(8,128)S(1)}, u32[]{:S(2)}, u32[]{:S(2)}) %all-to-all-start.1) | async-done | bytes 131104 | tf_op jit(solution)/shard_map/all_to_all | solution.py:477
  14.9 8.8 %z_gather.1 = bf16[16,24,5376]{2,1,0:T(8,128)(2,1)} custom-call(s32[16,16,128]{2,1,0:T(8,128)S(1)} %all-to-all-done.1.idx_ref, bf16[1,288,16384]{2,1,0:T(8,128)(2,1)} %props_ref.3, f32[4,512]{1,0:T(4,128)S(1)} %convolution_bitcast_fusion.after_ref.w_ref), custom_call_target="tpu_custom_call" | custom-call | flops 4831838208 | bytes 15000000 | tf_op jit(solution)/shard_map/z_gather/pallas_call | solution.py:499
  23.7 0.0 copy-start.3
  23.7 0.0 copy-start.4
  23.7 4.9 %all-to-all-start.2 = ((bf16[16,24,5376]{2,1,0:T(8,128)(2,1)}), bf16[16,24,5376]{2,1,0:T(8,128)(2,1)}, u32[]{:S(2)}, u32[]{:S(2)}) async-start(bf16[16,24,5376]{2,1,0:T(8,128)(2,1)} %z_gather.1), calls=%async_computation.2 | async-start | bytes 8257536 | tf_op jit(solution)/shard_map/all_to_all | solution.py:477
  28.6 0.7 slice.9.idx_ref
  29.3 0.0 copy-done.3
  29.4 0.5 weights.1.w_ref
  29.8 0.0 copy-done.4
  29.8 0.3 fusion.1
  30.1 0.7 compare_reduce_fusion
  31.4 13.1 %pair_pick.1.after_a.partner_ref = bf16[288,2048]{1,0:T(8,128)(2,1)S(1)} custom-call(s32[1]{0:T(128)} %bitcast.5.me_ref, s32[16,16,128]{2,1,0:T(8,128)S(1)} %all-to-all-done.1.idx_ref, bf16[1,288,16384]{2,1,0:T(8,128)(2,1)} %props_ref.3), custom_call_target="tpu_custom_call" | custom-call | flops 1207959552 | bytes 11000000 | tf_op jit(solution)/shard_map/pair_pick/pallas_call | solution.py:549
  44.5 33.2 %all-to-all-done.2.x_ref = bf16[16,24,5376]{2,1,0:T(8,128)(2,1)} async-done(((bf16[16,24,5376]{2,1,0:T(8,128)(2,1)}), bf16[16,24,5376]{2,1,0:T(8,128)(2,1)}, u32[]{:S(2)}, u32[]{:S(2)}) %all-to-all-start.2) | async-done | bytes 4128800 | tf_op jit(solution)/shard_map/all_to_all | solution.py:477
  78.4 0.0 copy-start.1
  78.5 0.0 copy-start.2
  78.5 9.4 %combo_sums.1 = s16[16,160,128]{2,1,0:T(8,128)(2,1)S(1)} custom-call(s32[1]{0:T(128)} %bitcast.3.more_ref, bf16[16,24,5376]{2,1,0:T(8,128)(2,1)} %all-to-all-done.2.x_ref, bf16[16,24,768]{2,1,0:T(8,128)(2,1)S(1)} %get-tuple-element.23.rest_ref, f32[4,6144]{1,0:T(4,128)S(1)} %weights.1.w_ref, bf16[288,2048]{1,0:T(8,128)(2,1)S(1)} %pair_pick.1.after_a.partner_ref, ...), custom_call_target="tpu_custom_call" | custom-call | flops 6341787648 | bytes 6000000 | tf_op jit(solution)/shard_map/combo_sums/pallas_call | solution.py:570
  87.9 15.4 %all_to_all.30.coded_ref = s16[16,160,128]{2,1,0:T(8,128)(2,1)S(1)} all-to-all(s16[16,160,128]{2,1,0:T(8,128)(2,1)S(1)} %combo_sums.1), channel_id=1, replica_groups=mesh['ta'=16,'sa'=8] {'ta'}, dimensions={0} | all-to-all | bytes 1310720 | tf_op jit(solution)/shard_map/all_to_all | solution.py:477
  103.3 0.5 reduce_sums.1
  103.8 15.2 %all_to_all.31.sums_ref = s16[8,160,128]{2,1,0:T(8,128)(2,1)S(1)} all-to-all(s16[8,160,128]{2,1,0:T(8,128)(2,1)S(1)} %reduce_sums.1), channel_id=1, replica_groups=mesh['ta'=16,'sa'=8] {'sa'}, dimensions={0} | all-to-all | bytes 655360 | tf_op jit(solution)/shard_map/all_to_all | solution.py:477
  119.0 0.0 copy-done.1
  119.0 0.0 copy-done.2
  119.0 1.9 %amplitudes.1 = f32[16,2,128]{2,1,0:T(2,128)S(1)} custom-call(s16[8,160,128]{2,1,0:T(8,128)(2,1)S(1)} %all_to_all.31.sums_ref, bf16[1024,64]{1,0:T(8,128)(2,1)S(1)} %copy-done.2, bf16[320,768]{1,0:T(8,128)(2,1)S(1)} %copy-done.1, bf16[288,2048]{1,0:T(8,128)(2,1)S(1)} %pair_pick.1.after_a.partner_ref), custom_call_target="tpu_custom_call" | custom-call | tf_op jit(solution)/shard_map/amplitudes/pallas_call | solution.py:606
  120.9 10.6 %all_to_all.32.back_ref = f32[16,2,128]{2,1,0:T(2,128)S(1)} all-to-all(f32[16,2,128]{2,1,0:T(2,128)S(1)} %amplitudes.1), channel_id=1, replica_groups=mesh['ta'=16,'sa'=8] {'ta'}, dimensions={0} | all-to-all | bytes 32768 | tf_op jit(solution)/shard_map/all_to_all | solution.py:477
  131.5 0.8 home.1
  (4 shorter events, 0.1 us)
Async XLA Ops:
  0.0 8.8 %copy-start = (f32[4,32]{1,0:T(4,128)S(1)}, f32[4,32]{1,0:T(4,128)}, u32[]{:S(2)}) copy-start(f32[4,32]{1,0:T(4,128)} %param.13) | copy-start | bytes 1540
  1.9 13.1 %all-to-all-start.1 = ((s32[16,16,128]{2,1,0:T(8,128)}), s32[16,16,128]{2,1,0:T(8,128)S(1)}, u32[]{:S(2)}, u32[]{:S(2)}) async-start(s32[16,16,128]{2,1,0:T(8,128)} %lists.1), calls=%async_computation.1 | async-start | bytes 262144 | tf_op jit(solution)/shard_map/all_to_all | solution.py:477
  23.7 5.7 %copy-start.3 = (s32[512]{0:T(512)S(1)}, s32[512]{0:T(512)}, u32[]{:S(2)}) copy-start(s32[512]{0:T(512)} %param.11) | copy-start | bytes 6148
  23.7 6.1 %copy-start.4 = (s32[512,1]{0,1:T(1,128)S(1)}, s32[512,1]{0,1:T(1,128)}, u32[]{:S(2)}) copy-start(s32[512,1]{0,1:T(1,128)} %param.14) | copy-start | bytes 6148
  23.7 54.0 %all-to-all-start.2 = ((bf16[16,24,5376]{2,1,0:T(8,128)(2,1)}), bf16[16,24,5376]{2,1,0:T(8,128)(2,1)}, u32[]{:S(2)}, u32[]{:S(2)}) async-start(bf16[16,24,5376]{2,1,0:T(8,128)(2,1)} %z_gather.1), calls=%async_computation.2 | async-start | bytes 8257536 | tf_op jit(solution)/shard_map/all_to_all | solution.py:477
  78.4 40.6 %copy-start.1 = (bf16[320,768]{1,0:T(8,128)(2,1)S(1)}, bf16[320,768]{1,0:T(8,128)(2,1)}, u32[]{:S(2)}) copy-start(bf16[320,768]{1,0:T(8,128)(2,1)} %constant.65.clone.spread_ref) | copy-start | bytes 1474564
  78.5 40.6 %copy-start.2 = (bf16[1024,64]{1,0:T(8,128)(2,1)S(1)}, bf16[1024,64]{1,0:T(8,128)(2,1)}, u32[]{:S(2)}) copy-start(bf16[1024,64]{1,0:T(8,128)(2,1)} %constant.64.clone.fold_ref) | copy-start | bytes 393220

commit v6 on v5

--- a/solution.py
+++ b/solution.py
@@ -261,7 +261,7 @@
 
 def combo_kernel(
     more_ref, x_ref, rest_ref, w_ref, after_a, after_b, after_c,
-    out_ref, held_ref, rest_held, acc_ref, last_ref, sums_ref, sems,
+    out_ref, held_ref, rest_held, acc_ref, sums_ref, sems,
 ):
     sources, _, lanes = x_ref.shape
     classes = w_ref.shape[0]
@@ -285,27 +285,32 @@
         left = jnp.concatenate(
             [scaled[c][n * t : n * t + n, :] for t in range(3) for c in range(classes)], axis=0
         ).astype(jnp.bfloat16)
-        contract = (((1,), (1,)), ((), ()))
-        main = lax.dot_general(left, right[0 : 2 * n], contract, preferred_element_type=jnp.float32)
-        last = lax.dot_general(
-            left[2 * classes * n :], right[2 * n :], contract, preferred_element_type=jnp.float32
-        )
-        return main, last
+        return [
+            lax.dot_general(
+                left[t * classes * n : (t + 1) * classes * n],
+                right[t * n : (t + 2) * n]
+                if t < 2
+                else jnp.concatenate([right[2 * n :], right[0:n]], axis=0),
+                (((1,), (1,)), ((), ())),
+                preferred_element_type=jnp.float32,
+            )
+            for t in range(3)
+        ]
 
     def chunk(s, carry):
         piece(s).wait()
         at = pl.ds(pl.multiple_of(s * depth, depth), depth)
-        main, last = products(held_ref[s].astype(jnp.float32), w_ref[:, at])
+        parts = products(held_ref[s].astype(jnp.float32), w_ref[:, at])
 
         @pl.when(s == 0)
         def _():
-            acc_ref[...] = main
-            last_ref[...] = last
+            for t in range(3):
+                acc_ref[t] = parts[t]
 
         @pl.when(s > 0)
         def _():
-            acc_ref[...] += main
-            last_ref[...] += last
+            for t in range(3):
+                acc_ref[t] += parts[t]
 
         return carry
 
@@ -316,9 +321,9 @@
         copy = pltpu.make_async_copy(rest_ref, rest_held, sems.at[lanes // depth])
         copy.start()
         copy.wait()
-        main, last = products(rest_held[...].astype(jnp.float32), w_ref[:, lanes : lanes + rest_depth])
-        acc_ref[...] += main
-        last_ref[...] += last
+        parts = products(rest_held[...].astype(jnp.float32), w_ref[:, lanes : lanes + rest_depth])
+        for t in range(3):
+            acc_ref[t] += parts[t]
 
     low_row = lax.broadcasted_iota(jnp.int32, (n, n), 0) % 8 < 4
     low_lane = lax.broadcasted_iota(jnp.int32, (n, n), 1) % 8 < 4
@@ -332,15 +337,16 @@
     for c in range(classes):
 
         def blk(left_tile, right_tile):
-            at = (left_tile * classes + c) * n
-            return acc_ref[at : at + n, n * right_tile : n * right_tile + n]
+            at = n * ((right_tile - left_tile) % 3)
+            return acc_ref[left_tile, c * n : c * n + n, at : at + n]
 
         re = (blk(0, 0) + blk(1, 1)).T
-        im = (blk(0, 1) - blk(1, 0)).T
-        a, b = blk(2, 0), swap_rows(blk(2, 1))
-        wide_col = jnp.where(low_row, a + b, b - a).T
+        im = blk(0, 1).T - blk(0, 1)
+        a, b = blk(2, 0).T, swap_lanes(blk(1, 2))
+        wide_col = jnp.where(low_lane, a + b, b - a)
+        a, b = blk(2, 0), swap_rows(blk(1, 2).T)
         tall_row = jnp.where(low_row, a + b, a - b)
-        a = last_ref[c * n : c * n + n, :]
+        a = blk(2, 2)
         b = swap_lanes(swap_rows(a))
         corner = jnp.where(low_row, jnp.where(low_lane, a + b, a - b), 0.0).T
         for k, m in enumerate((re, im, wide_col, tall_row, corner)):
@@ -581,8 +587,7 @@
         scratch_shapes=[
             pltpu.VMEM((3, slabs, 24, depth // 3), jnp.bfloat16),
             pltpu.VMEM((slabs, 24, rest_depth), jnp.bfloat16),
-            pltpu.VMEM((classes * slabs * 24, slabs * 16), jnp.float32),
-            pltpu.VMEM((classes * slabs * 8, slabs * 8), jnp.float32),
+            pltpu.VMEM((3, classes * slabs * 8, slabs * 16), jnp.float32),
             pltpu.VMEM((slabs, classes * 40, 128), jnp.float32),
             pltpu.SemaphoreType.DMA((4,)),
         ],

time: 133 us -> 131 us (0.985)
  Pallas kernels: 36.7 us -> 35.3 us
    pallas_call x1, Pallas kernels: 9.42 us -> 8.02 us  [local(): pl.pallas_call(combo_kernel, in_specs=[pl.BlockSpec(memory_space=pltpu.SM...]
where the time goes in v6:
time: 131 us
  blocking collectives  41.2 us (31%)
  waiting for transfers between devices  38.5 us (29%)
  Pallas kernels  35.3 us (27%)
  starting transfers between devices  11.9 us (9%)
  between operations  1.41 us (1%)
    all_to_all x3, blocking collectives, exchange(): return lax.all_to_all(array, axis, split_axis=0, concat_axis=0, tiled=True)  41.2 us
    all_to_all x2, waiting for transfers between devices, exchange(): return lax.all_to_all(array, axis, split_axis=0, concat_axis=0, tiled=True)  38.5 us
    pallas_call x1, Pallas kernels, local(): pl.pallas_call(pair_pick_kernel, in_specs=[pl.BlockSpec(memory_space=pltp...  13.1 us
    all_to_all x2, starting transfers between devices, exchange(): return lax.all_to_all(array, axis, split_axis=0, concat_axis=0, tiled=True)  11.9 us
    pallas_call x1, Pallas kernels, local(): pl.pallas_call(z_gather_kernel, in_specs=[IN_VMEM, pl.BlockSpec(memory_sp...  8.76 us
    pallas_call x1, Pallas kernels, local(): pl.pallas_call(combo_kernel, in_specs=[pl.BlockSpec(memory_space=pltpu.SM...  8.02 us
  transfers between devices with their start and end apart: 2, of which 2 were waited for; matrix products, arithmetic and copies ran while one was open for 2% of the time, Pallas kernels for 10%

profile of v6, /device:TPU:1, one launch (start us, length us, event | category | flops | bytes accessed | tf_op | source)
XLA Modules:
  0.0 130.8 jit_solution(13233432151836299528)
XLA Ops:
  0.0 0.0 copy-start
  0.0 1.8 %lists.1 = s32[16,16,128]{2,1,0:T(8,128)} custom-call(s32[4,128]{1,0:T(4,128)} %bitcast.28, s32[4,128]{1,0:T(4,128)} %bitcast.33, s32[4,128]{1,0:T(4,128)} %bitcast.30), custom_call_target="tpu_custom_call" | custom-call | tf_op jit(solution)/shard_map/lists/pallas_call | solution.py:486
  1.9 6.9 %all-to-all-start.1 = ((s32[16,16,128]{2,1,0:T(8,128)}), s32[16,16,128]{2,1,0:T(8,128)S(1)}, u32[]{:S(2)}, u32[]{:S(2)}) async-start(s32[16,16,128]{2,1,0:T(8,128)} %lists.1), calls=%async_computation.1 | async-start | bytes 262144 | tf_op jit(solution)/shard_map/all_to_all | solution.py:483
  8.8 0.0 copy-done
  8.8 0.8 convolution_bitcast_fusion.after_ref.w_ref
  9.6 5.3 %all-to-all-done.1.idx_ref = s32[16,16,128]{2,1,0:T(8,128)S(1)} async-done(((s32[16,16,128]{2,1,0:T(8,128)}), s32[16,16,128]{2,1,0:T(8,128)S(1)}, u32[]{:S(2)}, u32[]{:S(2)}) %all-to-all-start.1) | async-done | bytes 131104 | tf_op jit(solution)/shard_map/all_to_all | solution.py:483
  14.9 8.8 %z_gather.1 = bf16[16,24,5376]{2,1,0:T(8,128)(2,1)} custom-call(s32[16,16,128]{2,1,0:T(8,128)S(1)} %all-to-all-done.1.idx_ref, bf16[1,288,16384]{2,1,0:T(8,128)(2,1)} %props_ref.3, f32[4,512]{1,0:T(4,128)S(1)} %convolution_bitcast_fusion.after_ref.w_ref), custom_call_target="tpu_custom_call" | custom-call | flops 4831838208 | bytes 15000000 | tf_op jit(solution)/shard_map/z_gather/pallas_call | solution.py:505
  23.7 0.0 copy-start.3
  23.7 0.0 copy-start.4
  23.7 4.9 %all-to-all-start.2 = ((bf16[16,24,5376]{2,1,0:T(8,128)(2,1)}), bf16[16,24,5376]{2,1,0:T(8,128)(2,1)}, u32[]{:S(2)}, u32[]{:S(2)}) async-start(bf16[16,24,5376]{2,1,0:T(8,128)(2,1)} %z_gather.1), calls=%async_computation.2 | async-start | bytes 8257536 | tf_op jit(solution)/shard_map/all_to_all | solution.py:483
  28.6 0.7 slice.9.idx_ref
  29.3 0.0 copy-done.3
  29.4 0.5 weights.1.w_ref
  29.8 0.0 copy-done.4
  29.8 0.3 fusion.1
  30.1 0.7 compare_reduce_fusion
  31.4 13.1 %pair_pick.1.after_a.partner_ref = bf16[288,2048]{1,0:T(8,128)(2,1)S(1)} custom-call(s32[1]{0:T(128)} %bitcast.5.me_ref, s32[16,16,128]{2,1,0:T(8,128)S(1)} %all-to-all-done.1.idx_ref, bf16[1,288,16384]{2,1,0:T(8,128)(2,1)} %props_ref.3), custom_call_target="tpu_custom_call" | custom-call | flops 1207959552 | bytes 11000000 | tf_op jit(solution)/shard_map/pair_pick/pallas_call | solution.py:555
  44.5 33.2 %all-to-all-done.2.x_ref = bf16[16,24,5376]{2,1,0:T(8,128)(2,1)} async-done(((bf16[16,24,5376]{2,1,0:T(8,128)(2,1)}), bf16[16,24,5376]{2,1,0:T(8,128)(2,1)}, u32[]{:S(2)}, u32[]{:S(2)}) %all-to-all-start.2) | async-done | bytes 4128800 | tf_op jit(solution)/shard_map/all_to_all | solution.py:483
  78.4 0.0 copy-start.1
  78.5 0.0 copy-start.2
  78.5 8.0 %combo_sums.1 = s16[16,160,128]{2,1,0:T(8,128)(2,1)S(1)} custom-call(s32[1]{0:T(128)} %bitcast.3.more_ref, bf16[16,24,5376]{2,1,0:T(8,128)(2,1)} %all-to-all-done.2.x_ref, bf16[16,24,768]{2,1,0:T(8,128)(2,1)S(1)} %get-tuple-element.23.rest_ref, f32[4,6144]{1,0:T(4,128)S(1)} %weights.1.w_ref, bf16[288,2048]{1,0:T(8,128)(2,1)S(1)} %pair_pick.1.after_a.partner_ref, ...), custom_call_target="tpu_custom_call" | custom-call | flops 6341787648 | bytes 6000000 | tf_op jit(solution)/shard_map/combo_sums/pallas_call | solution.py:576
  86.5 15.4 %all_to_all.30.coded_ref = s16[16,160,128]{2,1,0:T(8,128)(2,1)S(1)} all-to-all(s16[16,160,128]{2,1,0:T(8,128)(2,1)S(1)} %combo_sums.1), channel_id=1, replica_groups=mesh['ta'=16,'sa'=8] {'ta'}, dimensions={0} | all-to-all | bytes 1310720 | tf_op jit(solution)/shard_map/all_to_all | solution.py:483
  101.9 0.5 reduce_sums.1
  102.4 15.2 %all_to_all.31.sums_ref = s16[8,160,128]{2,1,0:T(8,128)(2,1)S(1)} all-to-all(s16[8,160,128]{2,1,0:T(8,128)(2,1)S(1)} %reduce_sums.1), channel_id=1, replica_groups=mesh['ta'=16,'sa'=8] {'sa'}, dimensions={0} | all-to-all | bytes 655360 | tf_op jit(solution)/shard_map/all_to_all | solution.py:483
  117.6 0.0 copy-done.1
  117.6 0.0 copy-done.2
  117.6 1.9 %amplitudes.1 = f32[16,2,128]{2,1,0:T(2,128)S(1)} custom-call(s16[8,160,128]{2,1,0:T(8,128)(2,1)S(1)} %all_to_all.31.sums_ref, bf16[1024,64]{1,0:T(8,128)(2,1)S(1)} %copy-done.2, bf16[320,768]{1,0:T(8,128)(2,1)S(1)} %copy-done.1, bf16[288,2048]{1,0:T(8,128)(2,1)S(1)} %pair_pick.1.after_a.partner_ref), custom_call_target="tpu_custom_call" | custom-call | tf_op jit(solution)/shard_map/amplitudes/pallas_call | solution.py:611
  119.5 10.6 %all_to_all.32.back_ref = f32[16,2,128]{2,1,0:T(2,128)S(1)} all-to-all(f32[16,2,128]{2,1,0:T(2,128)S(1)} %amplitudes.1), channel_id=1, replica_groups=mesh['ta'=16,'sa'=8] {'ta'}, dimensions={0} | all-to-all | bytes 32768 | tf_op jit(solution)/shard_map/all_to_all | solution.py:483
  130.1 0.8 home.1
  (4 shorter events, 0.1 us)
Async XLA Ops:
  0.0 8.8 %copy-start = (f32[4,32]{1,0:T(4,128)S(1)}, f32[4,32]{1,0:T(4,128)}, u32[]{:S(2)}) copy-start(f32[4,32]{1,0:T(4,128)} %param.13) | copy-start | bytes 1540
  1.9 13.1 %all-to-all-start.1 = ((s32[16,16,128]{2,1,0:T(8,128)}), s32[16,16,128]{2,1,0:T(8,128)S(1)}, u32[]{:S(2)}, u32[]{:S(2)}) async-start(s32[16,16,128]{2,1,0:T(8,128)} %lists.1), calls=%async_computation.1 | async-start | bytes 262144 | tf_op jit(solution)/shard_map/all_to_all | solution.py:483
  23.7 5.7 %copy-start.3 = (s32[512]{0:T(512)S(1)}, s32[512]{0:T(512)}, u32[]{:S(2)}) copy-start(s32[512]{0:T(512)} %param.11) | copy-start | bytes 6148
  23.7 6.1 %copy-start.4 = (s32[512,1]{0,1:T(1,128)S(1)}, s32[512,1]{0,1:T(1,128)}, u32[]{:S(2)}) copy-start(s32[512,1]{0,1:T(1,128)} %param.14) | copy-start | bytes 6148
  23.7 54.0 %all-to-all-start.2 = ((bf16[16,24,5376]{2,1,0:T(8,128)(2,1)}), bf16[16,24,5376]{2,1,0:T(8,128)(2,1)}, u32[]{:S(2)}, u32[]{:S(2)}) async-start(bf16[16,24,5376]{2,1,0:T(8,128)(2,1)} %z_gather.1), calls=%async_computation.2 | async-start | bytes 8257536 | tf_op jit(solution)/shard_map/all_to_all | solution.py:483
  78.4 39.2 %copy-start.1 = (bf16[320,768]{1,0:T(8,128)(2,1)S(1)}, bf16[320,768]{1,0:T(8,128)(2,1)}, u32[]{:S(2)}) copy-start(bf16[320,768]{1,0:T(8,128)(2,1)} %constant.65.clone.spread_ref) | copy-start | bytes 1474564
  78.5 39.2 %copy-start.2 = (bf16[1024,64]{1,0:T(8,128)(2,1)S(1)}, bf16[1024,64]{1,0:T(8,128)(2,1)}, u32[]{:S(2)}) copy-start(bf16[1024,64]{1,0:T(8,128)(2,1)} %constant.64.clone.fold_ref) | copy-start | bytes 393220

commit v7 on v6

--- a/solution.py
+++ b/solution.py
@@ -127,48 +127,50 @@
 
 def z_gather_kernel(idx_ref, props_ref, after_ref, out_ref, block_ref, held_ref, in_sems, out_sems):
     slabs = out_ref.shape[0]
-    steps = block_ref.shape[0]
-    per = slabs // steps
-    lanes = block_ref.shape[2]
-    sites = lanes // per
-    ahead = min(3, steps)
-
-    def fetch(u):
-        at = pl.ds(pl.multiple_of(u * lanes, lanes), lanes)
-        return pltpu.make_async_copy(props_ref.at[0, :, at], block_ref.at[u], in_sems.at[u])
-
-    def send(u):
-        at = pl.ds(u * per, per)
-        return pltpu.make_async_copy(held_ref.at[at], out_ref.at[at], out_sems.at[u])
-
-    for u in range(ahead):
-        fetch(u).start()
-
-    def step(u, carry):
-        fetch(u).wait()
-
-        @pl.when(u + ahead < steps)
-        def _():
-            fetch(u + ahead).start()
-
-        for k in range(per):
-            t = u * per + k
-            idx = idx_ref[t]
-            rows = [idx[r : r + 1, :] for r in range(3)] + [doubled(idx[3:4, :], False)]
-            picked = pick_sites(block_ref[u, :, k * sites : (k + 1) * sites], rows)
-            for l in range(NSC):
-                held_ref[t, :, l * MAIN : (l + 1) * MAIN] = ordered_rows(picked[:, 0:MAIN], l).astype(
-                    jnp.bfloat16
-                )
-            for l in range(0, NSC, 2):
-                at = NSC * MAIN + 64 * l
-                held_ref[t, :, at : at + 128] = two_to_a_tile(picked[:, MAIN : MAIN + 128], l)
-        send(u).start()
-        return carry
-
-    lax.fori_loop(0, steps, step, 0)
-    for u in range(steps):
-        send(u).wait()
+    sites = props_ref.shape[2] // slabs
+    small, first, big = 2, 4, 4
+    stages = ((0, small, first // small), (first, big, (slabs - first) // big))
+
+    def fetch(at, number):
+        lanes = pl.ds(pl.multiple_of(at * sites, sites), number * sites)
+        return pltpu.make_async_copy(
+            props_ref.at[0, :, lanes], block_ref.at[:, lanes], in_sems.at[at]
+        )
+
+    def send(at, number):
+        part = pl.ds(at, number)
+        return pltpu.make_async_copy(held_ref.at[part], out_ref.at[part], out_sems.at[at])
+
+    for start, per, steps in stages:
+        for u in range(steps):
+            fetch(start + u * per, per).start()
+
+    for start, per, steps in stages:
+
+        def step(u, carry):
+            at = start + u * per
+            fetch(at, per).wait()
+            for k in range(per):
+                t = at + k
+                idx = idx_ref[t]
+                rows = [idx[r : r + 1, :] for r in range(3)] + [doubled(idx[3:4, :], False)]
+                lanes = pl.ds(pl.multiple_of(t * sites, sites), sites)
+                picked = pick_sites(block_ref[:, lanes], rows)
+                for l in range(NSC):
+                    held_ref[t, :, l * MAIN : (l + 1) * MAIN] = ordered_rows(
+                        picked[:, 0:MAIN], l
+                    ).astype(jnp.bfloat16)
+                for l in range(0, NSC, 2):
+                    to = NSC * MAIN + 64 * l
+                    held_ref[t, :, to : to + 128] = two_to_a_tile(picked[:, MAIN : MAIN + 128], l)
+            send(at, per).start()
+            return carry
+
+        lax.fori_loop(0, steps, step, 0)
+
+    for start, per, steps in stages:
+        for u in range(steps):
+            send(start + u * per, per).wait()
 
 
 def rest_gather_kernel(idx_ref, props_ref, out_ref):
@@ -215,8 +217,8 @@
 def coded(sums):
     groups, rows, lanes = sums.shape
     lane = lax.broadcasted_iota(jnp.int32, (groups, lanes), 1)
-    tail_row = lax.broadcasted_iota(jnp.int32, (groups, 16, lanes), 1)
-    tail = jnp.zeros((groups, 16, lanes), jnp.int32)
+    tail_row = lax.broadcasted_iota(jnp.int32, (groups, 8, lanes), 1)
+    tail = jnp.zeros((groups, 8, lanes), jnp.int32)
     whole, corners = [], []
     for c in range(rows // 40):
         part = sums[:, 40 * c : 40 * c + 40, :]
@@ -244,10 +246,10 @@
         value = coded_ref[g].astype(jnp.int32).astype(jnp.float32)
         rows, lanes = value.shape
         low = lax.broadcasted_iota(jnp.int32, (8, lanes), 1) % 8 < 4
-        classes = (rows - 16) // 36
+        classes = (rows - 8) // 36
         parts = []
         for c in range(classes):
-            scale = jnp.exp2(-value[rows - 16 + c : rows - 15 + c, :])
+            scale = jnp.exp2(-value[rows - 8 + c : rows - 7 + c, :])
             at = 32 * classes + 8 * (c // 2)
             corner = value[at : at + 8, :]
             if c % 2:
@@ -501,17 +503,16 @@
     ).astype(jnp.float32)
     weights = jnp.dot(kernel_table, one_hot, precision=lax.Precision.HIGHEST)
 
-    steps = slabs // 4
     z_rows = pl.pallas_call(
         z_gather_kernel,
         in_specs=[IN_VMEM, pl.BlockSpec(memory_space=pl.ANY), pl.BlockSpec(memory_space=pl.ANY)],
         out_specs=pl.BlockSpec(memory_space=pl.ANY),
         out_shape=jax.ShapeDtypeStruct((slabs, 24, depth), jnp.bfloat16),
         scratch_shapes=[
-            pltpu.VMEM((steps, rows, slabs // steps * site_count), jnp.bfloat16),
+            pltpu.VMEM((rows, slabs * site_count), jnp.bfloat16),
             pltpu.VMEM((slabs, 24, depth), jnp.bfloat16),
-            pltpu.SemaphoreType.DMA((steps,)),
-            pltpu.SemaphoreType.DMA((steps,)),
+            pltpu.SemaphoreType.DMA((slabs,)),
+            pltpu.SemaphoreType.DMA((slabs,)),
         ],
         compiler_params=params(50),
         cost_estimate=pl.CostEstimate(
@@ -583,7 +584,7 @@
         ]
         + [pl.BlockSpec(memory_space=pl.ANY)] * 3,
         out_specs=IN_VMEM,
-        out_shape=jax.ShapeDtypeStruct((slabs, classes * 36 + 16, 128), jnp.int16),
+        out_shape=jax.ShapeDtypeStruct((slabs, classes * 36 + 8, 128), jnp.int16),
         scratch_shapes=[
             pltpu.VMEM((3, slabs, 24, depth // 3), jnp.bfloat16),
             pltpu.VMEM((slabs, 24, rest_depth), jnp.bfloat16),

time: 131 us -> 131 us (level)
  no operation moved by 1% of the time
where the time goes in v7:
time: 131 us; the launch traced here: 130 us
  blocking collectives  40.7 us (31%)
  waiting for transfers between devices  38.5 us (29%)
  Pallas kernels  35.4 us (27%)
  starting transfers between devices  11.9 us (9%)
  between operations  1.41 us (1%)
    all_to_all x3, blocking collectives, exchange(): return lax.all_to_all(array, axis, split_axis=0, concat_axis=0, tiled=True)  40.7 us
    all_to_all x2, waiting for transfers between devices, exchange(): return lax.all_to_all(array, axis, split_axis=0, concat_axis=0, tiled=True)  38.5 us
    pallas_call x1, Pallas kernels, local(): pl.pallas_call(pair_pick_kernel, in_specs=[pl.BlockSpec(memory_space=pltp...  13.1 us
    all_to_all x2, starting transfers between devices, exchange(): return lax.all_to_all(array, axis, split_axis=0, concat_axis=0, tiled=True)  11.9 us
    pallas_call x1, Pallas kernels, local(): pl.pallas_call(z_gather_kernel, in_specs=[IN_VMEM, pl.BlockSpec(memory_sp...  8.81 us
    pallas_call x1, Pallas kernels, local(): pl.pallas_call(combo_kernel, in_specs=[pl.BlockSpec(memory_space=pltpu.SM...  8.01 us
  transfers between devices with their start and end apart: 2, of which 2 were waited for; matrix products, arithmetic and copies ran while one was open for 2% of the time, Pallas kernels for 10%

profile of v7, /device:TPU:1, one launch (start us, length us, event | category | flops | bytes accessed | tf_op | source)
XLA Modules:
  0.0 130.5 jit_solution(1691411491679264536)
XLA Ops:
  0.0 0.0 copy-start
  0.0 1.8 %lists.1 = s32[16,16,128]{2,1,0:T(8,128)} custom-call(s32[4,128]{1,0:T(4,128)} %bitcast.28, s32[4,128]{1,0:T(4,128)} %bitcast.33, s32[4,128]{1,0:T(4,128)} %bitcast.30), custom_call_target="tpu_custom_call" | custom-call | tf_op jit(solution)/shard_map/lists/pallas_call | solution.py:488
  1.9 6.9 %all-to-all-start.1 = ((s32[16,16,128]{2,1,0:T(8,128)}), s32[16,16,128]{2,1,0:T(8,128)S(1)}, u32[]{:S(2)}, u32[]{:S(2)}) async-start(s32[16,16,128]{2,1,0:T(8,128)} %lists.1), calls=%async_computation.1 | async-start | bytes 262144 | tf_op jit(solution)/shard_map/all_to_all | solution.py:485
  8.8 0.0 copy-done
  8.8 0.8 convolution_bitcast_fusion.after_ref.w_ref
  9.6 5.3 %all-to-all-done.1.idx_ref = s32[16,16,128]{2,1,0:T(8,128)S(1)} async-done(((s32[16,16,128]{2,1,0:T(8,128)}), s32[16,16,128]{2,1,0:T(8,128)S(1)}, u32[]{:S(2)}, u32[]{:S(2)}) %all-to-all-start.1) | async-done | bytes 131104 | tf_op jit(solution)/shard_map/all_to_all | solution.py:485
  14.9 8.8 %z_gather.1 = bf16[16,24,5376]{2,1,0:T(8,128)(2,1)} custom-call(s32[16,16,128]{2,1,0:T(8,128)S(1)} %all-to-all-done.1.idx_ref, bf16[1,288,16384]{2,1,0:T(8,128)(2,1)} %props_ref.3, f32[4,512]{1,0:T(4,128)S(1)} %convolution_bitcast_fusion.after_ref.w_ref), custom_call_target="tpu_custom_call" | custom-call | flops 4831838208 | bytes 15000000 | tf_op jit(solution)/shard_map/z_gather/pallas_call | solution.py:506
  23.7 0.0 copy-start.3
  23.8 0.0 copy-start.4
  23.8 4.9 %all-to-all-start.2 = ((bf16[16,24,5376]{2,1,0:T(8,128)(2,1)}), bf16[16,24,5376]{2,1,0:T(8,128)(2,1)}, u32[]{:S(2)}, u32[]{:S(2)}) async-start(bf16[16,24,5376]{2,1,0:T(8,128)(2,1)} %z_gather.1), calls=%async_computation.2 | async-start | bytes 8257536 | tf_op jit(solution)/shard_map/all_to_all | solution.py:485
  28.7 0.7 slice.9.idx_ref
  29.4 0.0 copy-done.3
  29.4 0.5 weights.1.w_ref
  29.9 0.0 copy-done.4
  29.9 0.3 fusion.1
  30.2 0.7 compare_reduce_fusion
  31.5 13.1 %pair_pick.1.after_a.partner_ref = bf16[288,2048]{1,0:T(8,128)(2,1)S(1)} custom-call(s32[1]{0:T(128)} %bitcast.5.me_ref, s32[16,16,128]{2,1,0:T(8,128)S(1)} %all-to-all-done.1.idx_ref, bf16[1,288,16384]{2,1,0:T(8,128)(2,1)} %props_ref.3), custom_call_target="tpu_custom_call" | custom-call | flops 1207959552 | bytes 11000000 | tf_op jit(solution)/shard_map/pair_pick/pallas_call | solution.py:556
  44.5 33.2 %all-to-all-done.2.x_ref = bf16[16,24,5376]{2,1,0:T(8,128)(2,1)} async-done(((bf16[16,24,5376]{2,1,0:T(8,128)(2,1)}), bf16[16,24,5376]{2,1,0:T(8,128)(2,1)}, u32[]{:S(2)}, u32[]{:S(2)}) %all-to-all-start.2) | async-done | bytes 4128800 | tf_op jit(solution)/shard_map/all_to_all | solution.py:485
  78.5 0.0 copy-start.1
  78.5 0.0 copy-start.2
  78.5 8.0 %combo_sums.1 = s16[16,152,128]{2,1,0:T(8,128)(2,1)S(1)} custom-call(s32[1]{0:T(128)} %bitcast.3.more_ref, bf16[16,24,5376]{2,1,0:T(8,128)(2,1)} %all-to-all-done.2.x_ref, bf16[16,24,768]{2,1,0:T(8,128)(2,1)S(1)} %get-tuple-element.23.rest_ref, f32[4,6144]{1,0:T(4,128)S(1)} %weights.1.w_ref, bf16[288,2048]{1,0:T(8,128)(2,1)S(1)} %pair_pick.1.after_a.partner_ref, ...), custom_call_target="tpu_custom_call" | custom-call | flops 6341787648 | bytes 6000000 | tf_op jit(solution)/shard_map/combo_sums/pallas_call | solution.py:577
  86.5 15.1 %all_to_all.30.coded_ref = s16[16,152,128]{2,1,0:T(8,128)(2,1)S(1)} all-to-all(s16[16,152,128]{2,1,0:T(8,128)(2,1)S(1)} %combo_sums.1), channel_id=1, replica_groups=mesh['ta'=16,'sa'=8] {'ta'}, dimensions={0} | all-to-all | bytes 1245184 | tf_op jit(solution)/shard_map/all_to_all | solution.py:485
  101.6 0.5 reduce_sums.1
  102.1 15.2 %all_to_all.31.sums_ref = s16[8,152,128]{2,1,0:T(8,128)(2,1)S(1)} all-to-all(s16[8,152,128]{2,1,0:T(8,128)(2,1)S(1)} %reduce_sums.1), channel_id=1, replica_groups=mesh['ta'=16,'sa'=8] {'sa'}, dimensions={0} | all-to-all | bytes 622592 | tf_op jit(solution)/shard_map/all_to_all | solution.py:485
  117.4 0.0 copy-done.1
  117.4 0.0 copy-done.2
  117.4 1.9 %amplitudes.1 = f32[16,2,128]{2,1,0:T(2,128)S(1)} custom-call(s16[8,152,128]{2,1,0:T(8,128)(2,1)S(1)} %all_to_all.31.sums_ref, bf16[1024,64]{1,0:T(8,128)(2,1)S(1)} %copy-done.2, bf16[320,768]{1,0:T(8,128)(2,1)S(1)} %copy-done.1, bf16[288,2048]{1,0:T(8,128)(2,1)S(1)} %pair_pick.1.after_a.partner_ref), custom_call_target="tpu_custom_call" | custom-call | tf_op jit(solution)/shard_map/amplitudes/pallas_call | solution.py:612
  119.3 10.4 %all_to_all.32.back_ref = f32[16,2,128]{2,1,0:T(2,128)S(1)} all-to-all(f32[16,2,128]{2,1,0:T(2,128)S(1)} %amplitudes.1), channel_id=1, replica_groups=mesh['ta'=16,'sa'=8] {'ta'}, dimensions={0} | all-to-all | bytes 32768 | tf_op jit(solution)/shard_map/all_to_all | solution.py:485
  129.7 0.8 home.1
  (4 shorter events, 0.1 us)
Async XLA Ops:
  0.0 8.8 %copy-start = (f32[4,32]{1,0:T(4,128)S(1)}, f32[4,32]{1,0:T(4,128)}, u32[]{:S(2)}) copy-start(f32[4,32]{1,0:T(4,128)} %param.13) | copy-start | bytes 1540
  1.9 13.1 %all-to-all-start.1 = ((s32[16,16,128]{2,1,0:T(8,128)}), s32[16,16,128]{2,1,0:T(8,128)S(1)}, u32[]{:S(2)}, u32[]{:S(2)}) async-start(s32[16,16,128]{2,1,0:T(8,128)} %lists.1), calls=%async_computation.1 | async-start | bytes 262144 | tf_op jit(solution)/shard_map/all_to_all | solution.py:485
  23.7 5.6 %copy-start.3 = (s32[512]{0:T(512)S(1)}, s32[512]{0:T(512)}, u32[]{:S(2)}) copy-start(s32[512]{0:T(512)} %param.11) | copy-start | bytes 6148
  23.8 6.1 %copy-start.4 = (s32[512,1]{0,1:T(1,128)S(1)}, s32[512,1]{0,1:T(1,128)}, u32[]{:S(2)}) copy-start(s32[512,1]{0,1:T(1,128)} %param.14) | copy-start | bytes 6148
  23.8 54.0 %all-to-all-start.2 = ((bf16[16,24,5376]{2,1,0:T(8,128)(2,1)}), bf16[16,24,5376]{2,1,0:T(8,128)(2,1)}, u32[]{:S(2)}, u32[]{:S(2)}) async-start(bf16[16,24,5376]{2,1,0:T(8,128)(2,1)} %z_gather.1), calls=%async_computation.2 | async-start | bytes 8257536 | tf_op jit(solution)/shard_map/all_to_all | solution.py:485
  78.5 38.9 %copy-start.1 = (bf16[320,768]{1,0:T(8,128)(2,1)S(1)}, bf16[320,768]{1,0:T(8,128)(2,1)}, u32[]{:S(2)}) copy-start(bf16[320,768]{1,0:T(8,128)(2,1)} %constant.65.clone.spread_ref) | copy-start | bytes 1474564
  78.5 38.9 %copy-start.2 = (bf16[1024,64]{1,0:T(8,128)(2,1)S(1)}, bf16[1024,64]{1,0:T(8,128)(2,1)}, u32[]{:S(2)}) copy-start(bf16[1024,64]{1,0:T(8,128)(2,1)} %constant.64.clone.fold_ref) | copy-start | bytes 393220
